TPU v7x, 32 devices: a whole 2x2x4 slice. The times are simulated.
32 devices in a mesh: space: 8 (over y, x, core), load: 4 (over z).
Axes of the slice: x: 2, y: 2, z: 4, core: 2. Of those that a mesh axis runs over, the one named last changes fastest.
Arguments:
- load_force: float32 [4, 3, 64, 16, 256], P('load', None, 'space'), may hold values from -6 to 6
- stiffness: float32 [64, 16, 256], P('space'), may hold values from 0.5 to 4
- material: int32 [8, 2], P('space'), may hold values from 0 to 2
- face_src: int32 [8, 8, 256], P('space'), may hold values from 0 to 32767
- face_count: int32 [8, 8], P('space'), may hold values from 0 to 256, as said below
- face_dst: int32 [8, 8, 256], P('space'), may hold values from 0 to 4095
Outputs:
- displacement: float32 [4, 3, 64, 16, 256], P('load', None, 'space')
- sensitivity: float32 [3, 64, 16, 256], P(None, 'space', 'load')
Inputs may be any that keep to these rules, and one draw needn't show every extreme that they name: face_count[s, o] counts the live first slots from slab s to owner o; in every row one owner gets all 256.
All inputs are finite; a program needn't handle non-finite values.
Results may differ from a plain program's by a relative error of at most 0.0001.
Values sent between devices are 32-bit elements; how exact they have to be, the bound alone decides.
A program may use at most 192 MiB of HBM per device.

v0:
```python
import jax
import jax.numpy as jnp
from jax import lax
from jax.sharding import PartitionSpec as P

NY = 16
BY = 8
SLOTS = 256
FINE_STEPS = 3
COARSE_STEPS = 4


UPPER_EDGE = 2.1
LOWER_EDGE = 0.15
COUPLING = 0.1
MODULI = (1.0, 0.55, 0.25)


def extended(block, sides, width):
    for axis, dim in sides:
        count = lax.axis_size(axis)
        forward = [(i, i + 1) for i in range(count - 1)]
        backward = [(target, source) for source, target in forward]
        low = lax.ppermute(
            lax.slice_in_dim(block, block.shape[dim] - width, None, axis=dim), axis, forward
        )
        high = lax.ppermute(lax.slice_in_dim(block, 0, width, axis=dim), axis, backward)
        block = jnp.concatenate([low, block, high], axis=dim)
    return block


def neighbour_list():
    entries = []
    for shift_x in (-1, 0, 1):
        for shift_y in (-1, 0, 1):
            for shift_z in (-1, 0, 1):
                reach_len = abs(shift_x) + abs(shift_y) + abs(shift_z)
                if reach_len > 0:
                    entries.append(
                        (shift_x, shift_y, shift_z, (1.0, 0.5, 0.25)[reach_len - 1] / 14.0)
                    )
    return entries


def window(padded, shift_x, shift_y, shift_z, inner_shape):
    size_x, size_y, size_z = inner_shape
    return padded[
        :,
        1 + shift_x : 1 + shift_x + size_x,
        1 + shift_y : 1 + shift_y + size_y,
        1 + shift_z : 1 + shift_z + size_z,
    ]


def operate(padded_field, padded_coef):
    inner_shape = (padded_field.shape[1] - 2, padded_field.shape[2] - 2, padded_field.shape[3] - 2)
    centre = window(padded_field, 0, 0, 0, inner_shape)
    coef_mid = window(padded_coef, 0, 0, 0, inner_shape)
    result = jnp.zeros_like(centre)
    for shift_x, shift_y, shift_z, weight in neighbour_list():
        face_coef = 0.5 * (coef_mid + window(padded_coef, shift_x, shift_y, shift_z, inner_shape))
        result = result + weight * face_coef * (
            centre - window(padded_field, shift_x, shift_y, shift_z, inner_shape)
        )
    pieces = []
    for component in range(3):
        mixed_term = jnp.zeros_like(coef_mid[0])
        for partner in range(3):
            if partner != component:
                for sign_a in (1, -1):
                    for sign_b in (1, -1):
                        offset = [0, 0, 0]
                        offset[component] += sign_a
                        offset[partner] += sign_b
                        mixed_term = (
                            mixed_term
                            + 0.25
                            * sign_a
                            * sign_b
                            * window(
                                padded_field[partner : partner + 1],
                                offset[0],
                                offset[1],
                                offset[2],
                                inner_shape,
                            )[0]
                        )
        pieces.append(result[component] - COUPLING * coef_mid[0] * mixed_term)
    return jnp.stack(pieces)


def diagonal_of(padded_coef):
    inner_shape = (padded_coef.shape[1] - 2, padded_coef.shape[2] - 2, padded_coef.shape[3] - 2)
    coef_mid = window(padded_coef, 0, 0, 0, inner_shape)
    total_sum = jnp.zeros_like(coef_mid)
    for shift_x, shift_y, shift_z, weight in neighbour_list():
        total_sum = total_sum + weight * 0.5 * (
            coef_mid + window(padded_coef, shift_x, shift_y, shift_z, inner_shape)
        )
    return total_sum


def pad_sides(grid_field):
    return jnp.pad(grid_field, ((0, 0), (0, 0), (1, 1), (1, 1)))


def chebyshev(source, padded_coef, diagonal, sweep_count, widen):
    midpoint = (UPPER_EDGE + LOWER_EDGE) / 2.0
    halfwidth = (UPPER_EDGE - LOWER_EDGE) / 2.0
    spread_ratio = midpoint / halfwidth
    rho_old = 1.0 / spread_ratio
    update = source / (midpoint * diagonal)
    solution = update
    for sweep_idx in range(1, sweep_count):
        residual = source - operate(widen(solution), padded_coef)
        rho_new = 1.0 / (2.0 * spread_ratio - rho_old)
        update = rho_new * rho_old * update + 2.0 * rho_new / halfwidth * residual / diagonal
        solution = solution + update
        rho_old = rho_new
    return solution


def coarsen(grid_field):
    comps, size_x, size_y, size_z = grid_field.shape
    return grid_field.reshape(comps, size_x // 2, 2, size_y // 2, 2, size_z // 2, 2).mean(
        axis=(2, 4, 6)
    )


def refine(grid_field):
    return jnp.repeat(jnp.repeat(jnp.repeat(grid_field, 2, axis=1), 2, axis=2), 2, axis=3)


def modulus_rows(material, brick_rows):
    onehot = (material[..., None] == jnp.arange(len(MODULI), dtype=jnp.int32)).astype(jnp.float32)
    values = jnp.sum(onehot * jnp.array(MODULI, jnp.float32), axis=-1)
    return jnp.repeat(values, brick_rows, axis=-1)


def widen_fine(grid_field):
    planes = extended(grid_field, (("space", 1),), 1)
    return pad_sides(planes)


def body(load_force, stiffness, material, face_src, face_count, face_dst):
    own_cells = modulus_rows(material, BY)[0][None, :, None]
    coef = stiffness * own_cells
    padded_coef = widen_fine(coef[None])
    diag_fine = diagonal_of(padded_coef)
    coarse_coef = coarsen(coef[None])

    def widen_coarse(grid_field):
        planes = extended(grid_field, (("space", 1),), 1)
        return pad_sides(planes)

    padded_coarse = widen_coarse(coarse_coef)
    diag_coarse = diagonal_of(padded_coarse)
    live_mask = (jnp.arange(SLOTS, dtype=jnp.int32)[None, :] < face_count[0][:, None]).astype(
        jnp.float32
    )
    source = load_force[0]
    smooth = chebyshev(source, padded_coef, diag_fine, FINE_STEPS, widen_fine)
    smooth, residual = (smooth, source - operate(widen_fine(smooth), padded_coef))
    coarse_source = 4.0 * coarsen(residual)
    picked = residual.reshape(3, -1)[:, face_src[0]] * live_mask[None]
    arrived = lax.all_to_all(picked, "space", split_axis=1, concat_axis=1, tiled=True)
    coarse_source = (
        coarse_source.reshape(3, -1).at[:, face_dst[0]].add(arrived).reshape(coarse_source.shape)
    )
    displaced = smooth + refine(
        chebyshev(coarse_source, padded_coarse, diag_coarse, COARSE_STEPS, widen_coarse)
    )
    image = operate(widen_fine(displaced), padded_coef)
    energy = jnp.sum(displaced * image, axis=0)
    outputs = [displaced]
    rows_part = NY // lax.axis_size("load")
    start_row = lax.axis_index("load") * rows_part
    total_sum = lax.psum(energy, "load")
    energy_part = lax.dynamic_slice_in_dim(total_sum, start_row, rows_part, 1)
    own_part = lax.dynamic_slice_in_dim(own_cells, start_row, rows_part, 1)[None]
    moduli = jnp.array(MODULI, jnp.float32)[:, None, None, None]
    sensitivity = (moduli - own_part) / own_part * energy_part[None]
    return (jnp.stack(outputs), sensitivity)


def solution(mesh):
    return jax.shard_map(
        body,
        mesh=mesh,
        in_specs=(
            P("load", None, "space", None, None),
            P("space", None, None),
            P("space", None),
            P("space", None, None),
            P("space", None),
            P("space", None, None),
        ),
        out_specs=(P("load", None, "space", None, None), P(None, "space", "load", None)),
        check_vma=False,
    )
```

profile of v0, /device:TPU:1, one launch (start us, length us, event | category | flops | bytes accessed | tf_op | source)
XLA Modules:
  0.0 330.7 jit_solution(5251915833790544887)
XLA Ops:
  11.2 4.5 %collective-permute-start = (f32[1,1,16,256]{3,2,1,0:T(8,128)S(1)}, f32[1,1,16,256]{3,2,1,0:T(8,128)S(1)}, u32[]{:S(2)}, u32[]{:S(2)}) collective-permute-start(f32[1,1,16,256]{3,2,1,0:T(8,128)S(1)} %get-tuple-element.68), channel_id=1, source_target_pairs={{0,4},{4,8},{8,12},{12,16},{16,20},{20,24},{24,28},{1,5},{5,9},{9,... | collective-permute-start | bytes 49160 | tf_op jit(solution)/shard_map/ppermute | solution.py:24
  16.6 9.8 %reshape_broadcast_in_dim.3 = f32[4,2,8,2,128,2]{5,4,3,2,1,0:T(8,128)} reshape(f32[8,16,256]{2,1,0:T(8,128)S(1)} %broadcast_multiply_fusion.1) | data formatting | bytes 262144 | tf_op jit(solution)/shard_map/reshape;broadcast_in_dim | solution.py:125
  26.4 4.1 %reduce_sum.38 = f32[4,8,128]{2,1,0:T(8,128)S(1)} reduce(f32[4,2,8,2,128,2]{5,4,3,2,1,0:T(8,128)} %reshape_broadcast_in_dim.3, f32[]{:T(128)} %constant.109.clone.1), dimensions={1,3,5}, to_apply=%region_3.4 | reduce | flops 28672 | bytes 147460 | tf_op jit(solution)/shard_map/reduce_sum | solution.py:125
  32.5 3.6 %collective-permute-start.8 = (f32[1,1,8,128]{3,2,1,0:T(8,128)S(1)}, f32[1,1,8,128]{3,2,1,0:T(8,128)S(1)}, u32[]{:S(2)}, u32[]{:S(2)}) collective-permute-start(f32[1,1,8,128]{3,2,1,0:T(8,128)S(1)} %get-tuple-element.102), channel_id=1, source_target_pairs={{0,4},{4,8},{8,12},{12,16},{16,20},{20,24},{24,28},{1,5},{5,9},{9,... | collective-permute-start | bytes 12296 | tf_op jit(solution)/shard_map/ppermute | solution.py:24
  37.4 26.5 %squeeze.11 = f32[3,4,2,8,2,128,2]{6,5,4,3,2,1,0:T(8,128)} reshape(f32[1,3,8,16,256]{4,3,2,1,0:T(8,128)S(1)} %copy-done) | data formatting | bytes 786432 | tf_op jit(solution)/shard_map/squeeze | solution.py:161
  64.0 8.6 %copy.310 = f32[1,3,8,16,256]{1,4,3,2,0:T(8,128)} copy(f32[1,3,8,16,256]{4,3,2,1,0:T(8,128)S(1)} %copy-done) | data formatting | bytes 786432 | tf_op args[0]
  76.8 3.6 %collective-permute-start.2 = (f32[3,1,16,256]{3,2,1,0:T(8,128)S(1)}, f32[3,1,16,256]{3,2,1,0:T(8,128)S(1)}, u32[]{:S(2)}, u32[]{:S(2)}) collective-permute-start(f32[3,1,16,256]{3,2,1,0:T(8,128)S(1)} %get-tuple-element.58), channel_id=1, source_target_pairs={{0,4},{4,8},{8,12},{12,16},{16,20},{20,24},{24,28},{1,5},{5,9},{9,... | collective-permute-start | bytes 147464 | tf_op jit(solution)/shard_map/ppermute | solution.py:24
  86.9 4.2 %collective-permute-start.4 = (f32[3,1,16,256]{3,2,1,0:T(8,128)S(1)}, f32[3,1,16,256]{3,2,1,0:T(8,128)S(1)}, u32[]{:S(2)}, u32[]{:S(2)}) collective-permute-start(f32[3,1,16,256]{3,2,1,0:T(8,128)S(1)} %get-tuple-element.56), channel_id=1, source_target_pairs={{0,4},{4,8},{8,12},{12,16},{16,20},{20,24},{24,28},{1,5},{5,9},{9,... | collective-permute-start | bytes 147464 | tf_op jit(solution)/shard_map/ppermute | solution.py:24
  97.7 4.4 %collective-permute-start.6 = (f32[3,1,16,256]{3,2,1,0:T(8,128)S(1)}, f32[3,1,16,256]{3,2,1,0:T(8,128)S(1)}, u32[]{:S(2)}, u32[]{:S(2)}) collective-permute-start(f32[3,1,16,256]{3,2,1,0:T(8,128)S(1)} %get-tuple-element.54), channel_id=1, source_target_pairs={{0,4},{4,8},{8,12},{12,16},{16,20},{20,24},{24,28},{1,5},{5,9},{9,... | collective-permute-start | bytes 147464 | tf_op jit(solution)/shard_map/ppermute | solution.py:24
  106.4 9.7 %stack.91 = f32[1,4,2,8,2,128,2]{6,5,4,3,2,1,0:T(8,128)} reshape(f32[1,8,16,256]{3,2,1,0:T(8,128)S(1)} %fusion.270) | data formatting | bytes 262144 | tf_op jit(solution)/shard_map/stack | solution.py:89
  116.2 9.7 %stack.90 = f32[1,4,2,8,2,128,2]{6,5,4,3,2,1,0:T(8,128)} reshape(f32[1,8,16,256]{3,2,1,0:T(8,128)S(1)} %get-tuple-element.23) | data formatting | bytes 262144 | tf_op jit(solution)/shard_map/stack | solution.py:89
  125.9 9.7 %stack.89 = f32[1,4,2,8,2,128,2]{6,5,4,3,2,1,0:T(8,128)} reshape(f32[1,8,16,256]{3,2,1,0:T(8,128)S(1)} %get-tuple-element.22) | data formatting | bytes 262144 | tf_op jit(solution)/shard_map/stack | solution.py:89
  136.4 8.6 %copy.311 = f32[3,32768]{0,1:T(8,128)} copy(f32[3,32768]{1,0:T(4,128)S(1)} %pad_maximum_fusion) | data formatting | bytes 786432 | tf_op jit(solution)/shard_map/stack | solution.py:89
  145.0 17.8 %bitcast_subtract_fusion = f32[3,32768]{0,1:T(8,128)} fusion(f32[3,32768]{0,1:T(8,128)} %copy.311, f32[1,3,8,16,256]{1,4,3,2,0:T(8,128)} %copy.310), kind=kLoop, calls=%fused_computation.4 | loop fusion | flops 98304 | bytes 1179648 | tf_op jit(solution)/shard_map/sub | solution.py:163
  162.8 11.2 %gather_fusion = f32[2048,3]{1,0:T(8,128)S(1)} fusion(f32[3,32768]{0,1:T(8,128)} %bitcast_subtract_fusion, s32[2048]{0:T(1024)S(1)} %copy-done.86), kind=kCustom, calls=%fused_computation | custom fusion | bytes 57344 | tf_op jit(solution)/shard_map/gather | solution.py:165
  175.0 9.4 %all-to-all-start = ((f32[3,8,256]{2,0,1:T(4,128)}), f32[3,8,256]{2,0,1:T(4,128)S(1)}, u32[]{:S(2)}, u32[]{:S(2)}) async-start(f32[3,8,256]{2,0,1:T(4,128)} %multiply_bitcast_fusion.1), calls=%async_computation | async-start | bytes 65536 | tf_op jit(solution)/shard_map/all_to_all | solution.py:166
  184.4 16.1 %fusion = f32[3,4,8,128]{3,2,1,0:T(8,128)S(1)} fusion(f32[3,4,2,8,2,128,2]{6,5,4,3,2,1,0:T(8,128)} %squeeze.11, f32[1,4,2,8,2,128,2]{6,5,4,3,2,1,0:T(8,128)} %stack.91, f32[1,4,2,8,2,128,2]{6,5,4,3,2,1,0:T(8,128)} %stack.90, f32[1,4,2,8,2,128,2]{6,5,4,3,2,1,0:T(8,128)} %stack.89), kind=kLoop, calls=%fused_computation.3 | loop fusion | flops 380928 | bytes 835584 | tf_op jit(solution)/shard_map/reduce_sum | solution.py:125
  202.5 12.6 %scatter_fusion = f32[3,4096]{0,1:T(8,128)S(1)} fusion(f32[3,4096]{0,1:T(8,128)S(1)} %bitcast.286, s32[2048]{0:T(1024)S(1)} %bitcast.312, f32[2048,3]{1,0:T(8,128)} %copy.313), kind=kCustom, calls=%fused_computation.1 | custom fusion | flops 6144 | bytes 81920 | tf_op jit(solution)/shard_map/scatter-add | solution.py:168
  218.0 3.8 %collective-permute-start.10 = (f32[3,1,8,128]{3,2,1,0:T(8,128)S(1)}, f32[3,1,8,128]{3,2,1,0:T(8,128)S(1)}, u32[]{:S(2)}, u32[]{:S(2)}) collective-permute-start(f32[3,1,8,128]{3,2,1,0:T(8,128)S(1)} %get-tuple-element.98), channel_id=1, source_target_pairs={{0,4},{4,8},{8,12},{12,16},{16,20},{20,24},{24,28},{1,5},{5,9},{9,... | collective-permute-start | bytes 36872 | tf_op jit(solution)/shard_map/ppermute | solution.py:24
  225.4 4.2 %collective-permute-start.12 = (f32[3,1,8,128]{3,2,1,0:T(8,128)S(1)}, f32[3,1,8,128]{3,2,1,0:T(8,128)S(1)}, u32[]{:S(2)}, u32[]{:S(2)}) collective-permute-start(f32[3,1,8,128]{3,2,1,0:T(8,128)S(1)} %get-tuple-element.96), channel_id=1, source_target_pairs={{0,4},{4,8},{8,12},{12,16},{16,20},{20,24},{24,28},{1,5},{5,9},{9,... | collective-permute-start | bytes 36872 | tf_op jit(solution)/shard_map/ppermute | solution.py:24
  233.1 4.2 %collective-permute-start.14 = (f32[3,1,8,128]{3,2,1,0:T(8,128)S(1)}, f32[3,1,8,128]{3,2,1,0:T(8,128)S(1)}, u32[]{:S(2)}, u32[]{:S(2)}) collective-permute-start(f32[3,1,8,128]{3,2,1,0:T(8,128)S(1)} %get-tuple-element.94), channel_id=1, source_target_pairs={{0,4},{4,8},{8,12},{12,16},{16,20},{20,24},{24,28},{1,5},{5,9},{9,... | collective-permute-start | bytes 36872 | tf_op jit(solution)/shard_map/ppermute | solution.py:24
  248.8 4.2 %collective-permute-start.16 = (f32[3,1,16,256]{3,2,1,0:T(8,128)}, f32[3,1,16,256]{3,2,1,0:T(8,128)}, u32[]{:S(2)}, u32[]{:S(2)}) collective-permute-start(f32[3,1,16,256]{3,2,1,0:T(8,128)} %get-tuple-element.52), channel_id=1, source_target_pairs={{0,4},{4,8},{8,12},{12,16},{16,20},{20,24},{24,28},{1,5},{5,9},{9,... | collective-permute-start | bytes 147464 | tf_op jit(solution)/shard_map/ppermute | solution.py:24
  256.6 3.3 %fusion.5 = f32[3,8,16,256]{3,2,1,0:T(8,128)S(1)} fusion(f32[3,8,16,256]{3,2,1,0:T(8,128)S(1)} %copy-done.6, f32[3,10,18,258]{3,2,1,0:T(8,128)S(1)} %select_maximum_fusion, f32[3,1,16,256]{3,2,1,0:T(8,128)} %collective-permute-done.17, f32[3,1,16,256]{3,2,1,0:T(8,128)} %collective-permute-done.16, f32[8,16,256]{2,1,0:T(8,128)} %copy-done.44, ...), kind=kLoop, calls=%fused_computation.31 | loop fusion | flops 7766016 | bytes 13729792 | tf_op jit(solution)/shard_map/add | solution.py:62
  264.1 57.1 %all-reduce.11.cloned.1.call-done = f32[8,16,256]{1,0,2:T(8,128)} async-done(((f32[8,16,256]{1,0,2:T(8,128)}), f32[8,16,256]{1,0,2:T(8,128)}) %all-reduce.11.cloned.1.call-update) | async-done | bytes 131088 | tf_op jit(solution)/shard_map/psum | solution.py:178
  (309 shorter events, 63.6 us)
Async XLA Ops:
  8.2 76.1 %copy-start.76 = (f32[16]{0:T(128)}, f32[16]{0:T(128)S(1)}, u32[]{:S(2)}) copy-start(f32[16]{0:T(128)S(1)} %broadcast_in_dim.30) | copy-start | bytes 196
  9.2 64.1 %collective-permute-start.1 = (f32[1,1,16,256]{3,2,1,0:T(8,128)S(1)}, f32[1,1,16,256]{3,2,1,0:T(8,128)S(1)}, u32[]{:S(2)}, u32[]{:S(2)}) collective-permute-start(f32[1,1,16,256]{3,2,1,0:T(8,128)S(1)} %get-tuple-element.69), channel_id=1, source_target_pairs={{4,0},{8,4},{12,8},{16,12},{20,16},{24,20},{28,24},{5,1},{9,5},{13... | collective-permute-start | bytes 49160 | tf_op jit(solution)/shard_map/ppermute | solution.py:27
  11.2 62.2 %collective-permute-start = (f32[1,1,16,256]{3,2,1,0:T(8,128)S(1)}, f32[1,1,16,256]{3,2,1,0:T(8,128)S(1)}, u32[]{:S(2)}, u32[]{:S(2)}) collective-permute-start(f32[1,1,16,256]{3,2,1,0:T(8,128)S(1)} %get-tuple-element.68), channel_id=1, source_target_pairs={{0,4},{4,8},{8,12},{12,16},{16,20},{20,24},{24,28},{1,5},{5,9},{9,... | collective-permute-start | bytes 49160 | tf_op jit(solution)/shard_map/ppermute | solution.py:24
  30.5 42.7 %collective-permute-start.9 = (f32[1,1,8,128]{3,2,1,0:T(8,128)S(1)}, f32[1,1,8,128]{3,2,1,0:T(8,128)S(1)}, u32[]{:S(2)}, u32[]{:S(2)}) collective-permute-start(f32[1,1,8,128]{3,2,1,0:T(8,128)S(1)} %get-tuple-element.103), channel_id=1, source_target_pairs={{4,0},{8,4},{12,8},{16,12},{20,16},{24,20},{28,24},{5,1},{9,5},{13... | collective-permute-start | bytes 12296 | tf_op jit(solution)/shard_map/ppermute | solution.py:27
  32.5 40.7 %collective-permute-start.8 = (f32[1,1,8,128]{3,2,1,0:T(8,128)S(1)}, f32[1,1,8,128]{3,2,1,0:T(8,128)S(1)}, u32[]{:S(2)}, u32[]{:S(2)}) collective-permute-start(f32[1,1,8,128]{3,2,1,0:T(8,128)S(1)} %get-tuple-element.102), channel_id=1, source_target_pairs={{0,4},{4,8},{8,12},{12,16},{16,20},{20,24},{24,28},{1,5},{5,9},{9,... | collective-permute-start | bytes 12296 | tf_op jit(solution)/shard_map/ppermute | solution.py:24
  74.1 29.4 %copy-start.15 = (f32[8,16,256]{2,1,0:T(8,128)}, f32[8,16,256]{2,1,0:T(8,128)S(1)}, u32[]{:S(2)}) copy-start(f32[8,16,256]{2,1,0:T(8,128)S(1)} %get-tuple-element.28) | copy-start | bytes 393220
  74.1 29.4 %copy-start.17 = (f32[8,16,256]{2,1,0:T(8,128)}, f32[8,16,256]{2,1,0:T(8,128)S(1)}, u32[]{:S(2)}) copy-start(f32[8,16,256]{2,1,0:T(8,128)S(1)} %get-tuple-element.29) | copy-start | bytes 393220
  74.1 29.4 %copy-start.19 = (f32[8,16,256]{2,1,0:T(8,128)}, f32[8,16,256]{2,1,0:T(8,128)S(1)}, u32[]{:S(2)}) copy-start(f32[8,16,256]{2,1,0:T(8,128)S(1)} %get-tuple-element.30) | copy-start | bytes 393220
  74.9 5.9 %collective-permute-start.3 = (f32[3,1,16,256]{3,2,1,0:T(8,128)S(1)}, f32[3,1,16,256]{3,2,1,0:T(8,128)S(1)}, u32[]{:S(2)}, u32[]{:S(2)}) collective-permute-start(f32[3,1,16,256]{3,2,1,0:T(8,128)S(1)} %get-tuple-element.59), channel_id=1, source_target_pairs={{4,0},{8,4},{12,8},{16,12},{20,16},{24,20},{28,24},{5,1},{9,5},{13... | collective-permute-start | bytes 147464 | tf_op jit(solution)/shard_map/ppermute | solution.py:27
  76.8 4.8 %collective-permute-start.2 = (f32[3,1,16,256]{3,2,1,0:T(8,128)S(1)}, f32[3,1,16,256]{3,2,1,0:T(8,128)S(1)}, u32[]{:S(2)}, u32[]{:S(2)}) collective-permute-start(f32[3,1,16,256]{3,2,1,0:T(8,128)S(1)} %get-tuple-element.58), channel_id=1, source_target_pairs={{0,4},{4,8},{8,12},{12,16},{16,20},{20,24},{24,28},{1,5},{5,9},{9,... | collective-permute-start | bytes 147464 | tf_op jit(solution)/shard_map/ppermute | solution.py:24
  84.9 7.0 %collective-permute-start.5 = (f32[3,1,16,256]{3,2,1,0:T(8,128)S(1)}, f32[3,1,16,256]{3,2,1,0:T(8,128)S(1)}, u32[]{:S(2)}, u32[]{:S(2)}) collective-permute-start(f32[3,1,16,256]{3,2,1,0:T(8,128)S(1)} %get-tuple-element.57), channel_id=1, source_target_pairs={{4,0},{8,4},{12,8},{16,12},{20,16},{24,20},{28,24},{5,1},{9,5},{13... | collective-permute-start | bytes 147464 | tf_op jit(solution)/shard_map/ppermute | solution.py:27
  86.9 5.4 %collective-permute-start.4 = (f32[3,1,16,256]{3,2,1,0:T(8,128)S(1)}, f32[3,1,16,256]{3,2,1,0:T(8,128)S(1)}, u32[]{:S(2)}, u32[]{:S(2)}) collective-permute-start(f32[3,1,16,256]{3,2,1,0:T(8,128)S(1)} %get-tuple-element.56), channel_id=1, source_target_pairs={{0,4},{4,8},{8,12},{12,16},{16,20},{20,24},{24,28},{1,5},{5,9},{9,... | collective-permute-start | bytes 147464 | tf_op jit(solution)/shard_map/ppermute | solution.py:24
  95.7 7.1 %collective-permute-start.7 = (f32[3,1,16,256]{3,2,1,0:T(8,128)S(1)}, f32[3,1,16,256]{3,2,1,0:T(8,128)S(1)}, u32[]{:S(2)}, u32[]{:S(2)}) collective-permute-start(f32[3,1,16,256]{3,2,1,0:T(8,128)S(1)} %get-tuple-element.55), channel_id=1, source_target_pairs={{4,0},{8,4},{12,8},{16,12},{20,16},{24,20},{28,24},{5,1},{9,5},{13... | collective-permute-start | bytes 147464 | tf_op jit(solution)/shard_map/ppermute | solution.py:27
  97.7 5.4 %collective-permute-start.6 = (f32[3,1,16,256]{3,2,1,0:T(8,128)S(1)}, f32[3,1,16,256]{3,2,1,0:T(8,128)S(1)}, u32[]{:S(2)}, u32[]{:S(2)}) collective-permute-start(f32[3,1,16,256]{3,2,1,0:T(8,128)S(1)} %get-tuple-element.54), channel_id=1, source_target_pairs={{0,4},{4,8},{8,12},{12,16},{16,20},{20,24},{24,28},{1,5},{5,9},{9,... | collective-permute-start | bytes 147464 | tf_op jit(solution)/shard_map/ppermute | solution.py:24
  175.0 26.2 %all-to-all-start = ((f32[3,8,256]{2,0,1:T(4,128)}), f32[3,8,256]{2,0,1:T(4,128)S(1)}, u32[]{:S(2)}, u32[]{:S(2)}) async-start(f32[3,8,256]{2,0,1:T(4,128)} %multiply_bitcast_fusion.1), calls=%async_computation | async-start | bytes 65536 | tf_op jit(solution)/shard_map/all_to_all | solution.py:166
  184.4 136.8 %all-reduce.11.cloned.1.call-start = ((), (), s32[]{:S(2)}) async-start(), calls=%async_computation.1 | async-start | bytes 2097152 | tf_op jit(solution)/shard_map/psum | solution.py:178
  216.0 5.9 %collective-permute-start.11 = (f32[3,1,8,128]{3,2,1,0:T(8,128)S(1)}, f32[3,1,8,128]{3,2,1,0:T(8,128)S(1)}, u32[]{:S(2)}, u32[]{:S(2)}) collective-permute-start(f32[3,1,8,128]{3,2,1,0:T(8,128)S(1)} %get-tuple-element.99), channel_id=1, source_target_pairs={{4,0},{8,4},{12,8},{16,12},{20,16},{24,20},{28,24},{5,1},{9,5},{13... | collective-permute-start | bytes 36872 | tf_op jit(solution)/shard_map/ppermute | solution.py:27
  218.0 4.4 %collective-permute-start.10 = (f32[3,1,8,128]{3,2,1,0:T(8,128)S(1)}, f32[3,1,8,128]{3,2,1,0:T(8,128)S(1)}, u32[]{:S(2)}, u32[]{:S(2)}) collective-permute-start(f32[3,1,8,128]{3,2,1,0:T(8,128)S(1)} %get-tuple-element.98), channel_id=1, source_target_pairs={{0,4},{4,8},{8,12},{12,16},{16,20},{20,24},{24,28},{1,5},{5,9},{9,... | collective-permute-start | bytes 36872 | tf_op jit(solution)/shard_map/ppermute | solution.py:24
  223.5 6.1 %collective-permute-start.13 = (f32[3,1,8,128]{3,2,1,0:T(8,128)S(1)}, f32[3,1,8,128]{3,2,1,0:T(8,128)S(1)}, u32[]{:S(2)}, u32[]{:S(2)}) collective-permute-start(f32[3,1,8,128]{3,2,1,0:T(8,128)S(1)} %get-tuple-element.97), channel_id=1, source_target_pairs={{4,0},{8,4},{12,8},{16,12},{20,16},{24,20},{28,24},{5,1},{9,5},{13... | collective-permute-start | bytes 36872 | tf_op jit(solution)/shard_map/ppermute | solution.py:27
  225.4 5.0 %collective-permute-start.12 = (f32[3,1,8,128]{3,2,1,0:T(8,128)S(1)}, f32[3,1,8,128]{3,2,1,0:T(8,128)S(1)}, u32[]{:S(2)}, u32[]{:S(2)}) collective-permute-start(f32[3,1,8,128]{3,2,1,0:T(8,128)S(1)} %get-tuple-element.96), channel_id=1, source_target_pairs={{0,4},{4,8},{8,12},{12,16},{16,20},{20,24},{24,28},{1,5},{5,9},{9,... | collective-permute-start | bytes 36872 | tf_op jit(solution)/shard_map/ppermute | solution.py:24
  231.1 6.8 %collective-permute-start.15 = (f32[3,1,8,128]{3,2,1,0:T(8,128)S(1)}, f32[3,1,8,128]{3,2,1,0:T(8,128)S(1)}, u32[]{:S(2)}, u32[]{:S(2)}) collective-permute-start(f32[3,1,8,128]{3,2,1,0:T(8,128)S(1)} %get-tuple-element.95), channel_id=1, source_target_pairs={{4,0},{8,4},{12,8},{16,12},{20,16},{24,20},{28,24},{5,1},{9,5},{13... | collective-permute-start | bytes 36872 | tf_op jit(solution)/shard_map/ppermute | solution.py:27
  233.1 5.0 %collective-permute-start.14 = (f32[3,1,8,128]{3,2,1,0:T(8,128)S(1)}, f32[3,1,8,128]{3,2,1,0:T(8,128)S(1)}, u32[]{:S(2)}, u32[]{:S(2)}) collective-permute-start(f32[3,1,8,128]{3,2,1,0:T(8,128)S(1)} %get-tuple-element.94), channel_id=1, source_target_pairs={{0,4},{4,8},{8,12},{12,16},{16,20},{20,24},{24,28},{1,5},{5,9},{9,... | collective-permute-start | bytes 36872 | tf_op jit(solution)/shard_map/ppermute | solution.py:24
  246.9 8.1 %collective-permute-start.17 = (f32[3,1,16,256]{3,2,1,0:T(8,128)}, f32[3,1,16,256]{3,2,1,0:T(8,128)}, u32[]{:S(2)}, u32[]{:S(2)}) collective-permute-start(f32[3,1,16,256]{3,2,1,0:T(8,128)} %get-tuple-element.53), channel_id=1, source_target_pairs={{4,0},{8,4},{12,8},{16,12},{20,16},{24,20},{28,24},{5,1},{9,5},{13... | collective-permute-start | bytes 147464 | tf_op jit(solution)/shard_map/ppermute | solution.py:27
  248.8 6.2 %collective-permute-start.16 = (f32[3,1,16,256]{3,2,1,0:T(8,128)}, f32[3,1,16,256]{3,2,1,0:T(8,128)}, u32[]{:S(2)}, u32[]{:S(2)}) collective-permute-start(f32[3,1,16,256]{3,2,1,0:T(8,128)} %get-tuple-element.52), channel_id=1, source_target_pairs={{0,4},{4,8},{8,12},{12,16},{16,20},{20,24},{24,28},{1,5},{5,9},{9,... | collective-permute-start | bytes 147464 | tf_op jit(solution)/shard_map/ppermute | solution.py:24
  (91 other events, 1006.8 us)
Sparse Core Ops, SparseCore 0:
  264.1 56.9 all-reduce.10
where the time goes:
time: 332 us; the launch traced here: 331 us
  local copies, waits for them, and re-layouts  112 us (34%)
  other arithmetic  79.5 us (24%)
  starting transfers between devices  63.6 us (19%)
  waiting for transfers between devices  59.9 us (18%)
  between operations  16 us (5%)
    psum x1, waiting for transfers between devices, body(): total_sum = lax.psum(energy, 'load')  57.1 us
    another operation x4, local copies, waits for them, and re-layouts, operate(): return jnp.stack(pieces)  37.8 us
    ppermute x9, starting transfers between devices, extended(): lax.ppermute(lax.slice_in_dim(block, block.shape[dim] - width, None, axis...  36.8 us
    squeeze x1, local copies, waits for them, and re-layouts, body(): source = load_force[0]  26.5 us
    reduce_sum x2, other arithmetic, coarsen(): grid_field.reshape(comps, size_x // 2, 2, size_y // 2, 2, size_z // 2, 2)  20.2 us
    sub x1, other arithmetic, body(): source - operate(widen_fine(smooth), padded_coef)  17.8 us
    ppermute x9, starting transfers between devices, extended(): lax.ppermute(lax.slice_in_dim(block, 0, width, axis=dim), axis, backward)  17.4 us
    unnamed x197, local copies, waits for them, and re-layouts  13.1 us
  transfers between devices with their start and end apart: 20, of which 7 were waited for; matrix products, arithmetic and copies ran while one was open for 22% of the time, Pallas kernels for 0%

commit v1 on v0

v1 whole, which is shorter than its diff:
```python
import functools

import jax
import jax.numpy as jnp
from jax import lax
from jax.experimental import pallas as pl
from jax.experimental.pallas import tpu as pltpu
from jax.sharding import PartitionSpec as P

BY = 8
FINE_STEPS = 3
COARSE_STEPS = 4
UPPER_EDGE = 2.1
LOWER_EDGE = 0.15
COUPLING = 0.1
MODULI = (1.0, 0.55, 0.25)

MID = (UPPER_EDGE + LOWER_EDGE) / 2.0
HALF = (UPPER_EDGE - LOWER_EDGE) / 2.0
F32 = jnp.float32
BF16 = jnp.bfloat16
MESH = pl.DeviceIdType.MESH
FH = 4
CH = 4


def cheb_factors(count):
    spread = MID / HALF
    rho = 1.0 / spread
    out = []
    for _ in range(1, count):
        rho_new = 1.0 / (2.0 * spread - rho)
        out.append((rho_new * rho, 2.0 * rho_new / HALF))
        rho = rho_new
    return out


def split(x):
    hi = x.astype(BF16)
    return hi, (x - hi.astype(F32)).astype(BF16)


def dot2(x, table):
    hi, lo = split(x)
    return jnp.dot(hi, table, preferred_element_type=F32) + jnp.dot(
        lo, table, preferred_element_type=F32
    )


class Plane:
    def __init__(self, rows, lanes):
        self.rows, self.lanes = rows, lanes
        row = lax.broadcasted_iota(jnp.int32, (rows, lanes), 0)
        lane = lax.broadcasted_iota(jnp.int32, (rows, lanes), 1)
        self.masks = (row == rows - 1, row == 0, lane == lanes - 1, lane == 0)

    def yp(self, a):
        return jnp.where(self.masks[0], 0.0, pltpu.roll(a, self.rows - 1, 0))

    def ym(self, a):
        return jnp.where(self.masks[1], 0.0, pltpu.roll(a, 1, 0))

    def zp(self, a):
        return jnp.where(self.masks[2], 0.0, pltpu.roll(a, self.lanes - 1, 1))

    def zm(self, a):
        return jnp.where(self.masks[3], 0.0, pltpu.roll(a, 1, 1))

    def ty(self, a):
        return a + 0.5 * (self.yp(a) + self.ym(a))

    def tz(self, a):
        return a + 0.5 * (self.zp(a) + self.zm(a))

    def apply(self, v, w, coef, p):
        u0 = [v[c, p] for c in range(3)]
        um = [v[c, p - 1] for c in range(3)]
        up = [v[c, p + 1] for c in range(3)]
        a = [(u0[c] + 0.5 * (um[c] + up[c])) * (1.0 / 14.0) for c in range(3)]
        e = [(up[c] - um[c]) * (0.5 * COUPLING) for c in range(3)]
        b = [(w[c, p] + 0.5 * (w[c, p - 1] + w[c, p + 1])) * (1.0 / 14.0) for c in range(3)]
        half = 0.5 * COUPLING
        t = self.ty(a[0])
        mix_x = (
            t
            + 0.5 * (self.zp(t + e[2]) + self.zm(t - e[2]))
            + 0.5 * (self.yp(e[1]) - self.ym(e[1]))
        )
        t = self.tz(a[1])
        g = e[0] + half * (self.zp(u0[2]) - self.zm(u0[2]))
        mix_y = t + 0.5 * (self.yp(t + g) + self.ym(t - g))
        t = self.ty(a[2])
        g = e[0] + half * (self.yp(u0[1]) - self.ym(u0[1]))
        mix_z = t + 0.5 * (self.zp(t + g) + self.zm(t - g))
        k, dk = coef[0, p], coef[1, p]
        mix = (mix_x, mix_y, mix_z)
        return [dk * u0[c] - k * mix[c] - self.tz(self.ty(b[c])) for c in range(3)]

    def diag(self, k, p):
        t = k[p] + 0.5 * (k[p - 1] + k[p + 1])
        return (3.0 / 7.0) * k[p] + self.tz(self.ty(t)) * (1.0 / 14.0)


def planes_loop(low, high, unroll, step):
    def run(p, carry):
        step(p)
        return carry

    lax.fori_loop(low, high, run, 0, unroll=unroll)


def start_sweep(low, high, unroll, src, coef, d, v, w):
    def step(p):
        scale = coef[2, p] * (1.0 / MID)
        k = coef[0, p]
        for c in range(3):
            new = src[c, p] * scale
            d[c, p] = new
            v[c, p] = new
            w[c, p] = k * new

    planes_loop(low, high, unroll, step)


def sweep(plane, low, high, unroll, factors, src, coef, d, v, w, v_out, w_out):
    alpha, beta = factors

    def step(p):
        image = plane.apply(v, w, coef, p)
        k = coef[0, p]
        scale = coef[2, p] * beta
        for c in range(3):
            new = alpha * d[c, p] + scale * (src[c, p] - image[c])
            d[c, p] = new
            total = v[c, p] + new
            v_out[c, p] = total
            w_out[c, p] = k * total

    planes_loop(low, high, unroll, step)


def kernel(
    n, loads,
    force, stiff, mat, face_src, count, face_dst,
    disp_out, sens_out,
    src, raw, coef, d, va, wa, vb, wb, res, pooled, kc, ccoef, csrc, cd, cva, cwa, cvb, cwb,
    wide, sendbuf, arrived, esend, erecv,
    local_sem, send_sem, recv_sem, a_send, a_recv, e_send, e_recv,
):
    me = lax.axis_index("space")
    load = lax.axis_index("load")
    cx, ny, nz = raw.shape
    hx, hy, hz = cx // 2, ny // 2, nz // 2
    fine = Plane(ny, nz)
    coarse = Plane(hy, hz)
    slots = face_src.shape[2]
    top = cx + 2 * FH
    ctop = hx + 2 * CH

    barrier = pltpu.get_barrier_semaphore()

    @pl.loop(1, n)
    def _(k):
        pl.semaphore_signal(
            barrier, inc=1, device_id={"space": lax.rem(me + k, n)}, device_id_type=MESH
        )

    @pl.loop(1, loads)
    def _(k):
        pl.semaphore_signal(
            barrier, inc=1, device_id={"load": lax.rem(load + k, loads)}, device_id_type=MESH
        )

    get_stiff = pltpu.make_async_copy(stiff, raw, local_sem.at[0])
    get_force = pltpu.make_async_copy(force.at[0], src.at[:, pl.ds(FH, cx)], local_sem.at[1])
    get_stiff.start()
    get_force.start()

    right = lax.rem(me + 1, n)
    left = lax.rem(me + n - 1, n)

    def pair(kind, to_right, to_left):
        made = []
        for side, (ends, target) in enumerate(((to_right, right), (to_left, left))):
            made.append(
                pltpu.make_async_remote_copy(
                    src_ref=ends[0], dst_ref=ends[1],
                    send_sem=send_sem.at[kind, side], recv_sem=recv_sem.at[kind, side],
                    device_id={"space": target}, device_id_type=MESH,
                )
            )
        return made

    fw = FH - 1
    force_pair = pair(
        0,
        (force.at[0, :, pl.ds(cx - fw, fw)], src.at[:, pl.ds(1, fw)]),
        (force.at[0, :, pl.ds(0, fw)], src.at[:, pl.ds(FH + cx, fw)]),
    )
    coef_pair = pair(
        1,
        (coef.at[0, pl.ds(cx, FH)], coef.at[0, pl.ds(0, FH)]),
        (coef.at[0, pl.ds(FH, FH)], coef.at[0, pl.ds(FH + cx, FH)]),
    )
    ccoef_pair = pair(
        2,
        (ccoef.at[:, pl.ds(CH, hx)], ccoef.at[:, pl.ds(0, hx)]),
        (ccoef.at[:, pl.ds(CH, hx)], ccoef.at[:, pl.ds(CH + hx, hx)]),
    )
    csrc_pair = pair(
        3,
        (csrc.at[:, pl.ds(CH, hx)], csrc.at[:, pl.ds(0, hx)]),
        (csrc.at[:, pl.ds(CH, hx)], csrc.at[:, pl.ds(CH + hx, hx)]),
    )
    has_left, has_right = me > 0, me < n - 1

    def start(made):
        @pl.when(has_right)
        def _():
            made[0].start()

        @pl.when(has_left)
        def _():
            made[1].start()

    def land(made):
        @pl.when(has_left)
        def _():
            made[0].wait_recv()

        @pl.when(has_right)
        def _():
            made[1].wait_recv()

    def sent(made):
        @pl.when(has_right)
        def _():
            made[0].wait_send()

        @pl.when(has_left)
        def _():
            made[1].wait_send()

    @pl.when(me == 0)
    def _():
        src[:, 0:FH] = jnp.zeros((3, FH, ny, nz), F32)
        coef[0, 0:FH] = jnp.zeros((FH, ny, nz), F32)
        ccoef[:, 0:CH] = jnp.zeros((3, CH, hy, hz), F32)
        csrc[:, 0:CH] = jnp.zeros((3, CH, hy, hz), F32)

    @pl.when(me == n - 1)
    def _():
        src[:, FH + cx : top] = jnp.zeros((3, FH, ny, nz), F32)
        coef[0, FH + cx : top] = jnp.zeros((FH, ny, nz), F32)
        ccoef[:, CH + hx : ctop] = jnp.zeros((3, CH, hy, hz), F32)
        csrc[:, CH + hx : ctop] = jnp.zeros((3, CH, hy, hz), F32)

    def by_material(brick, values):
        m = mat[0, brick]
        return jnp.where(m == 0, values[0], jnp.where(m == 1, values[1], values[2]))

    get_stiff.wait()
    for brick in range(ny // BY):
        own = by_material(brick, MODULI)
        rows = slice(brick * BY, (brick + 1) * BY)
        coef[0, FH : FH + cx, rows] = raw[:, rows] * own

    pl.semaphore_wait(barrier, n - 1 + loads - 1)
    start(coef_pair)
    start(force_pair)

    pool = (
        lax.shift_right_logical(lax.broadcasted_iota(jnp.int32, (nz, hz), 0), 1)
        == lax.broadcasted_iota(jnp.int32, (nz, hz), 1)
    ).astype(F32).astype(BF16)
    spread = (
        lax.shift_right_logical(lax.broadcasted_iota(jnp.int32, (hz, nz), 1), 1)
        == lax.broadcasted_iota(jnp.int32, (hz, nz), 0)
    ).astype(F32).astype(BF16)

    def pool_rows(i):
        return pooled[i, pl.ds(0, hy, stride=2), :] + pooled[i, pl.ds(1, hy, stride=2), :]

    land(coef_pair)
    kview = coef.at[0]

    def diag_step(p):
        diag = fine.diag(kview, p)
        inside = jnp.logical_and(
            jnp.logical_or(p >= FH, has_left), jnp.logical_or(p < FH + cx, has_right)
        )
        keep = jnp.where(inside, 1.0, 0.0)
        coef[1, p] = diag + coef[0, p] * (1.0 / 7.0)
        coef[2, p] = keep / jnp.where(inside, diag, 1.0)

    planes_loop(1, top - 1, 1, diag_step)

    count_c = hx + 2
    first = FH - 2
    stack = jnp.concatenate(
        [coef[0, first + 2 * i] + coef[0, first + 2 * i + 1] for i in range(count_c)], axis=0
    )
    pooled[0:count_c] = dot2(stack, pool).reshape(count_c, ny, hz)
    for i in range(count_c):
        kc[i] = pool_rows(i) * 0.125
    for i in range(hx):
        diag = coarse.diag(kc, i + 1)
        ccoef[0, CH + i] = kc[i + 1]
        ccoef[1, CH + i] = diag + kc[i + 1] * (1.0 / 7.0)
        ccoef[2, CH + i] = 1.0 / diag
    start(ccoef_pair)

    get_force.wait()
    land(force_pair)

    factors = cheb_factors(FINE_STEPS)
    start_sweep(1, top - 1, 2, src, coef, d, va, wa)
    sweep(fine, 2, top - 2, 1, factors[0], src, coef, d, va, wa, vb, wb)
    sweep(fine, 3, top - 3, 1, factors[1], src, coef, d, vb, wb, va, wa)

    def residual_step(p):
        image = fine.apply(va, wa, coef, p)
        for c in range(3):
            res[c, p - FH] = src[c, p] - image[c]

    planes_loop(FH, FH + cx, 1, residual_step)

    rows_f = cx * ny
    flat = res[...].reshape(3 * rows_f, nz)
    flat_hi, flat_lo = split(flat)
    wide[0] = flat_hi
    wide[1] = flat_lo
    zbits = nz.bit_length() - 1
    hbits = hz.bit_length() - 1
    sub_z = lax.broadcasted_iota(jnp.int32, (nz, slots), 0)
    sub_r = lax.broadcasted_iota(jnp.int32, (rows_f, slots), 0)
    slot_r = lax.broadcasted_iota(jnp.int32, (rows_f, slots), 1)

    def pick(owner):
        index = face_src[0, pl.ds(owner, 1), :]
        lanes = (sub_z == jnp.bitwise_and(index, nz - 1)).astype(F32).astype(BF16)
        found = jnp.dot(wide[0], lanes, preferred_element_type=F32) + jnp.dot(
            wide[1], lanes, preferred_element_type=F32
        )
        live = jnp.logical_and(
            sub_r == lax.shift_right_logical(index, zbits), slot_r < count[0, owner]
        )
        return [
            jnp.sum(
                jnp.where(live, found[c * rows_f : (c + 1) * rows_f], 0.0), axis=0, keepdims=True
            )
            for c in range(3)
        ]

    def a_copy(k):
        owner = lax.rem(me + k, n)
        return pltpu.make_async_remote_copy(
            src_ref=sendbuf.at[owner], dst_ref=arrived.at[me],
            send_sem=a_send.at[k], recv_sem=a_recv.at[k],
            device_id={"space": owner}, device_id_type=MESH,
        )

    zero_tail = jnp.zeros((5, slots), F32)

    @pl.loop(1, n)
    def _(k):
        owner = lax.rem(me + k, n)
        sendbuf[owner] = jnp.concatenate(pick(owner) + [zero_tail], axis=0)
        a_copy(k).start()

    arrived[me] = jnp.concatenate(pick(me) + [zero_tail], axis=0)

    for c in range(3):
        stack = jnp.concatenate([res[c, 2 * i] + res[c, 2 * i + 1] for i in range(hx)], axis=0)
        pooled[0:hx] = dot2(stack, pool).reshape(hx, ny, hz)
        for i in range(hx):
            csrc[c, CH + i] = pool_rows(i) * 0.5

    rows_c = hx * hy
    sub_l = lax.broadcasted_iota(jnp.int32, (hz, slots), 0)
    sub_c = lax.broadcasted_iota(jnp.int32, (rows_c, slots), 0)

    def place(sender):
        index = face_dst[0, pl.ds(sender, 1), :]
        lanes = (sub_l == jnp.bitwise_and(index, hz - 1)).astype(F32).astype(BF16)
        at_row = sub_c == lax.shift_right_logical(index, hbits)
        values = arrived[sender]
        parts = [jnp.where(at_row, values[c : c + 1], 0.0) for c in range(3)]
        hi, lo = split(jnp.concatenate(parts, axis=0))
        dims = (((1,), (1,)), ((), ()))
        return lax.dot_general(hi, lanes, dims, preferred_element_type=F32) + lax.dot_general(
            lo, lanes, dims, preferred_element_type=F32
        )

    def add_sender(k, total):
        a_copy(k).wait_recv()
        return total + place(lax.rem(me + n - k, n))

    total = lax.fori_loop(1, n, add_sender, place(me))
    csrc[:, CH : CH + hx] += total.reshape(3, hx, hy, hz)
    start(csrc_pair)
    land(ccoef_pair)
    land(csrc_pair)

    factors = cheb_factors(COARSE_STEPS)
    start_sweep(0, ctop, 2, csrc, ccoef, cd, cva, cwa)
    sweep(coarse, 1, ctop - 1, 2, factors[0], csrc, ccoef, cd, cva, cwa, cvb, cwb)
    sweep(coarse, 2, ctop - 2, 2, factors[1], csrc, ccoef, cd, cvb, cwb, cva, cwa)
    sweep(coarse, 3, ctop - 3, 2, factors[2], csrc, ccoef, cd, cva, cwa, cvb, cwb)

    fresh = hx + 2
    for c in range(3):
        lifted = dot2(cvb[c, 3 : 3 + fresh].reshape(fresh * hy, hz), spread)
        for i in range(fresh):
            plane = lifted[i * hy : (i + 1) * hy]
            doubled = jnp.broadcast_to(plane[:, None, :], (hy, 2, nz)).reshape(ny, nz)
            for p in (FH - 2 + 2 * i, FH - 1 + 2 * i):
                if FH - 1 <= p <= FH + cx:
                    vb[c, p] = va[c, p] + doubled
                    wb[c, p] = coef[0, p] * vb[c, p]

    put_disp = pltpu.make_async_copy(
        vb.at[:, pl.ds(FH, cx)], disp_out.at[0], local_sem.at[2]
    )
    put_disp.start()

    part = ny // loads

    def energy_step(p):
        image = fine.apply(vb, wb, coef, p)
        energy = vb[0, p] * image[0] + vb[1, p] * image[1] + vb[2, p] * image[2]
        for i in range(loads):
            esend[i, p - FH] = energy[i * part : (i + 1) * part]

    planes_loop(FH, FH + cx, 1, energy_step)

    def e_copy(k):
        owner = lax.rem(load + k, loads)
        return pltpu.make_async_remote_copy(
            src_ref=esend.at[owner], dst_ref=erecv.at[k],
            send_sem=e_send.at[k], recv_sem=e_recv.at[k],
            device_id={"load": owner}, device_id_type=MESH,
        )

    for k in range(1, loads):
        e_copy(k).start()

    sent(force_pair)
    sent(coef_pair)
    sent(ccoef_pair)
    sent(csrc_pair)

    @pl.loop(1, n)
    def _(k):
        a_copy(k).wait_send()

    total = esend[load]
    for k in range(1, loads):
        e_copy(k).wait_recv()
        total = total + erecv[k]
    brick = (load * part) // BY
    for m, modulus in enumerate(MODULI):
        ratio = by_material(brick, [(modulus - own) / own for own in MODULI])
        sens_out[m] = total * ratio
    for k in range(1, loads):
        e_copy(k).wait_send()
    put_disp.wait()


def body(n, loads, load_force, stiffness, material, face_src, face_count, face_dst):
    cx, ny, nz = stiffness.shape
    hx, hy, hz = cx // 2, ny // 2, nz // 2
    slots = face_src.shape[2]
    part = ny // loads
    fine = (cx + 2 * FH, ny, nz)
    coarse = (hx + 2 * CH, hy, hz)
    vmem = pl.BlockSpec(memory_space=pltpu.VMEM)
    smem = pl.BlockSpec(memory_space=pltpu.SMEM)
    hbm = pl.BlockSpec(memory_space=pl.ANY)

    def buf(*shape):
        return pltpu.VMEM(shape, F32)

    dma = pltpu.SemaphoreType.DMA
    return pl.pallas_call(
        functools.partial(kernel, n, loads),
        out_shape=(
            jax.ShapeDtypeStruct(load_force.shape, F32),
            jax.ShapeDtypeStruct((3, cx, part, nz), F32),
        ),
        in_specs=[hbm, hbm, smem, vmem, smem, vmem],
        out_specs=(hbm, vmem),
        scratch_shapes=[
            buf(3, *fine), buf(cx, ny, nz), buf(3, *fine), buf(3, *fine),
            buf(3, *fine), buf(3, *fine), buf(3, *fine), buf(3, *fine),
            buf(3, cx, ny, nz), buf(hx + 2, ny, hz), buf(hx + 2, hy, hz),
            buf(3, *coarse), buf(3, *coarse), buf(3, *coarse),
            buf(3, *coarse), buf(3, *coarse), buf(3, *coarse), buf(3, *coarse),
            pltpu.VMEM((2, 3 * cx * ny, nz), BF16),
            buf(n, 8, slots), buf(n, 8, slots),
            buf(loads, cx, part, nz), buf(loads, cx, part, nz),
            dma((3,)), dma((4, 2)), dma((4, 2)),
            dma((n,)), dma((n,)), dma((loads,)), dma((loads,)),
        ],
        compiler_params=pltpu.CompilerParams(
            collective_id=0, has_side_effects=True, vmem_limit_bytes=40 * 1024 * 1024
        ),
    )(load_force, stiffness, material, face_src, face_count, face_dst)


def solution(mesh):
    return jax.shard_map(
        functools.partial(body, mesh.shape["space"], mesh.shape["load"]),
        mesh=mesh,
        in_specs=(
            P("load", None, "space", None, None),
            P("space", None, None),
            P("space", None),
            P("space", None, None),
            P("space", None),
            P("space", None, None),
        ),
        out_specs=(P("load", None, "space", None, None), P(None, "space", "load", None)),
        check_vma=False,
    )
```

time: 332 us -> 37.7 us (0.11)
  local copies, waits for them, and re-layouts: 112 us -> 5.98 us
  other arithmetic: 79.5 us -> 0 us
  starting transfers between devices: 63.6 us -> 0 us
  waiting for transfers between devices: 59.9 us -> 0 us
  Pallas kernels: 0 us -> 30.7 us
  between operations: 16 us -> 0.65 us
    psum x1 -> x0, waiting for transfers between devices: 57.1 us -> none  [body(): total_sum = lax.psum(energy, 'load')]
    ppermute x18 -> x0, starting transfers between devices: 54.2 us -> none  [the longest x9 36.8 us: extended(): lax.ppermute(lax.slice_in_dim(block, block.shape[dim] - width, None, axis...]
    another operation x5 -> x0, local copies, waits for them, and re-layouts: 47.6 us -> none  [the longest x4 37.8 us: operate(): return jnp.stack(pieces)]
    pallas_call x0 -> x1, Pallas kernels: none -> 30.7 us  [body(): pl.pallas_call(functools.partial(kernel, n, loads), out_shape=(jax.ShapeD...]
    squeeze x1 -> x0, local copies, waits for them, and re-layouts: 26.5 us -> none  [body(): source = load_force[0]]
    reduce_sum x4 -> x0, other arithmetic: 22 us -> none  [the longest x2 20.2 us: coarsen(): grid_field.reshape(comps, size_x // 2, 2, size_y // 2, 2, size_z // 2, 2)]
    sub x13 -> x0, other arithmetic: 20.6 us -> none  [the longest x1 17.8 us: body(): source - operate(widen_fine(smooth), padded_coef)]
    scatter-add x1 -> x0, other arithmetic: 12.6 us -> none  [body(): coarse_source.reshape(3, -1).at[:, face_dst[0]].add(arrived)]
  transfers between devices with their start and end apart: 20 -> 0, of which waited for: 7 -> 0; matrix products, arithmetic and copies ran while one was open for 22% -> 0% of each run, Pallas kernels for 0% -> 0%
where the time goes in v1:
time: 37.7 us; the launch traced here: 37.4 us
  Pallas kernels  30.7 us (81%)
  local copies, waits for them, and re-layouts  5.98 us (16%)
  between operations  0.65 us (2%)
    pallas_call x1, Pallas kernels, body(): pl.pallas_call(functools.partial(kernel, n, loads), out_shape=(jax.ShapeD...  30.7 us
    unnamed x14, local copies, waits for them, and re-layouts  5.98 us

profile of v1, /device:TPU:1, one launch (start us, length us, event | category | flops | bytes accessed | tf_op | source)
XLA Modules:
  0.0 37.4 jit_solution(2043803576915180335)
XLA Ops:
  0.6 0.0 copy-start
  0.6 1.0 %copy-done = f32[1,3,8,16,256]{4,3,2,1,0:T(8,128)S(1)} copy-done((f32[1,3,8,16,256]{4,3,2,1,0:T(8,128)S(1)}, f32[1,3,8,16,256]{4,3,2,1,0:T(8,128)}, u32[]{:S(2)}) %copy-start) | copy-done | bytes 393240
  1.6 0.0 copy-start.1
  1.6 0.9 %copy-done.1 = f32[8,16,256]{2,1,0:T(8,128)S(1)} copy-done((f32[8,16,256]{2,1,0:T(8,128)S(1)}, f32[8,16,256]{2,1,0:T(8,128)}, u32[]{:S(2)}) %copy-start.1) | copy-done | bytes 131096
  2.5 0.0 copy-start.2
  2.5 0.7 %copy-done.2 = s32[1,8,256]{2,1,0:T(8,128)S(1)} copy-done((s32[1,8,256]{2,1,0:T(8,128)S(1)}, s32[1,8,256]{2,1,0:T(8,128)}, u32[]{:S(2)}) %copy-start.2) | copy-done | bytes 8216
  3.2 0.0 copy-start.3
  3.2 0.7 %copy-done.3 = s32[1,8,256]{2,1,0:T(8,128)S(1)} copy-done((s32[1,8,256]{2,1,0:T(8,128)S(1)}, s32[1,8,256]{2,1,0:T(8,128)}, u32[]{:S(2)}) %copy-start.3) | copy-done | bytes 8216
  3.9 0.0 copy-start.4
  3.9 0.7 %copy-done.4 = s32[1,2]{1,0:T(1,128)S(1)} copy-done((s32[1,2]{1,0:T(1,128)S(1)}, s32[1,2]{1,0:T(1,128)}, u32[]{:S(2)}) %copy-start.4) | copy-done | bytes 32
  4.6 0.0 copy-start.5
  4.6 0.7 %copy-done.5 = s32[1,8]{1,0:T(1,128)S(1)} copy-done((s32[1,8]{1,0:T(1,128)S(1)}, s32[1,8]{1,0:T(1,128)}, u32[]{:S(2)}) %copy-start.5) | copy-done | bytes 56
  5.2 30.7 %shard_map.77 = (f32[1,3,8,16,256]{4,3,2,1,0:T(8,128)S(1)}, f32[3,8,4,256]{3,2,1,0:T(4,128)S(1)}) custom-call(f32[1,3,8,16,256]{4,3,2,1,0:T(8,128)S(1)} %copy-done, f32[8,16,256]{2,1,0:T(8,128)S(1)} %copy-done.1, s32[1,2]{1,0:T(1,128)S(1)} %copy-done.4, s32[1,8,256]{2,1,0:T(8,128)S(1)} %copy-done.2, s32[1,8]{1,0:T(1,128)S(1)} %copy-done.5, ...), custom_call_target="tpu_custom_call" | custom-call | tf_op jit(solution)/shard_map/pallas_call | solution.py:485
  36.0 0.7 %copy.10 = f32[1,3,8,16,256]{4,3,2,1,0:T(8,128)} copy(f32[1,3,8,16,256]{4,3,2,1,0:T(8,128)S(1)} %get-tuple-element.4) | data formatting | bytes 786432
  36.7 0.6 %copy.11 = f32[3,8,4,256]{3,2,1,0:T(4,128)} copy(f32[3,8,4,256]{3,2,1,0:T(4,128)S(1)} %get-tuple-element.5) | data formatting | bytes 196608
Async XLA Ops:
  0.6 1.0 %copy-start = (f32[1,3,8,16,256]{4,3,2,1,0:T(8,128)S(1)}, f32[1,3,8,16,256]{4,3,2,1,0:T(8,128)}, u32[]{:S(2)}) copy-start(f32[1,3,8,16,256]{4,3,2,1,0:T(8,128)} %force.1) | copy-start | bytes 1179652
  1.6 0.9 %copy-start.1 = (f32[8,16,256]{2,1,0:T(8,128)S(1)}, f32[8,16,256]{2,1,0:T(8,128)}, u32[]{:S(2)}) copy-start(f32[8,16,256]{2,1,0:T(8,128)} %stiff.1) | copy-start | bytes 393220
  2.5 0.7 %copy-start.2 = (s32[1,8,256]{2,1,0:T(8,128)S(1)}, s32[1,8,256]{2,1,0:T(8,128)}, u32[]{:S(2)}) copy-start(s32[1,8,256]{2,1,0:T(8,128)} %face_src.1) | copy-start | bytes 24580
  3.2 0.7 %copy-start.3 = (s32[1,8,256]{2,1,0:T(8,128)S(1)}, s32[1,8,256]{2,1,0:T(8,128)}, u32[]{:S(2)}) copy-start(s32[1,8,256]{2,1,0:T(8,128)} %face_dst.1) | copy-start | bytes 24580
  3.9 0.7 %copy-start.4 = (s32[1,2]{1,0:T(1,128)S(1)}, s32[1,2]{1,0:T(1,128)}, u32[]{:S(2)}) copy-start(s32[1,2]{1,0:T(1,128)} %mat.1) | copy-start | bytes 28
  4.6 0.7 %copy-start.5 = (s32[1,8]{1,0:T(1,128)S(1)}, s32[1,8]{1,0:T(1,128)}, u32[]{:S(2)}) copy-start(s32[1,8]{1,0:T(1,128)} %count.1) | copy-start | bytes 100

commit v2 on v1

--- a/solution.py
+++ b/solution.py
@@ -101,7 +101,19 @@
         return (3.0 / 7.0) * k[p] + self.tz(self.ty(t)) * (1.0 / 14.0)
 
 
-def planes_loop(low, high, unroll, step):
+def planes_loop(planes, step):
+    if isinstance(planes, list):
+        low, other, count = planes
+
+        def run(i, carry):
+            step(low + i)
+            step(other + i)
+            return carry
+
+        lax.fori_loop(0, count, run, 0)
+        return
+    low, high, unroll = planes
+
     def run(p, carry):
         step(p)
         return carry
@@ -109,7 +121,7 @@
     lax.fori_loop(low, high, run, 0, unroll=unroll)
 
 
-def start_sweep(low, high, unroll, src, coef, d, v, w):
+def start_sweep(planes, src, coef, d, v, w):
     def step(p):
         scale = coef[2, p] * (1.0 / MID)
         k = coef[0, p]
@@ -119,10 +131,10 @@
             v[c, p] = new
             w[c, p] = k * new
 
-    planes_loop(low, high, unroll, step)
-
-
-def sweep(plane, low, high, unroll, factors, src, coef, d, v, w, v_out, w_out):
+    planes_loop(planes, step)
+
+
+def sweep(plane, planes, factors, src, coef, d, v, w, v_out, w_out):
     alpha, beta = factors
 
     def step(p):
@@ -136,14 +148,15 @@
             v_out[c, p] = total
             w_out[c, p] = k * total
 
-    planes_loop(low, high, unroll, step)
+    planes_loop(planes, step)
 
 
 def kernel(
     n, loads,
-    force, stiff, mat, face_src, count, face_dst,
+    force, stiff, mat_hbm, face_src_hbm, count_hbm, face_dst_hbm,
     disp_out, sens_out,
     src, raw, coef, d, va, wa, vb, wb, res, pooled, kc, ccoef, csrc, cd, cva, cwa, cvb, cwb,
+    mat, face_src, count, face_dst, lane_table, live_table, dst_table,
     wide, sendbuf, arrived, esend, erecv,
     local_sem, send_sem, recv_sem, a_send, a_recv, e_send, e_recv,
 ):
@@ -173,8 +186,16 @@
 
     get_stiff = pltpu.make_async_copy(stiff, raw, local_sem.at[0])
     get_force = pltpu.make_async_copy(force.at[0], src.at[:, pl.ds(FH, cx)], local_sem.at[1])
+    get_mat = pltpu.make_async_copy(mat_hbm, mat, local_sem.at[3])
+    get_src = pltpu.make_async_copy(face_src_hbm, face_src, local_sem.at[4])
+    get_count = pltpu.make_async_copy(count_hbm, count, local_sem.at[5])
+    get_dst = pltpu.make_async_copy(face_dst_hbm, face_dst, local_sem.at[6])
     get_stiff.start()
+    get_mat.start()
     get_force.start()
+    get_src.start()
+    get_count.start()
+    get_dst.start()
 
     right = lax.rem(me + 1, n)
     left = lax.rem(me + n - 1, n)
@@ -259,6 +280,7 @@
         m = mat[0, brick]
         return jnp.where(m == 0, values[0], jnp.where(m == 1, values[1], values[2]))
 
+    get_mat.wait()
     get_stiff.wait()
     for brick in range(ny // BY):
         own = by_material(brick, MODULI)
@@ -268,6 +290,97 @@
     pl.semaphore_wait(barrier, n - 1 + loads - 1)
     start(coef_pair)
     start(force_pair)
+
+    rows_f = cx * ny
+    zbits = nz.bit_length() - 1
+    hbits = hz.bit_length() - 1
+    get_src.wait()
+    get_count.wait()
+    get_dst.wait()
+
+    @pl.loop(0, n)
+    def _(owner):
+        sub_z = lax.broadcasted_iota(jnp.int32, (nz, slots), 0)
+        sub_r = lax.broadcasted_iota(jnp.int32, (rows_f, slots), 0)
+        slot_r = lax.broadcasted_iota(jnp.int32, (rows_f, slots), 1)
+        index = face_src[0, pl.ds(owner, 1), :]
+        lane_table[owner] = (sub_z == jnp.bitwise_and(index, nz - 1)).astype(F32).astype(BF16)
+        live = jnp.logical_and(
+            sub_r == lax.shift_right_logical(index, zbits), slot_r < count[0, owner]
+        )
+        live_table[owner] = live.astype(F32)
+        sub_l = lax.broadcasted_iota(jnp.int32, (hz, slots), 0)
+        index = face_dst[0, pl.ds(owner, 1), :]
+        dst_table[owner] = (sub_l == jnp.bitwise_and(index, hz - 1)).astype(F32).astype(BF16)
+
+    kview = coef.at[0]
+
+    def diag_step(p):
+        diag = fine.diag(kview, p)
+        inside = jnp.logical_and(
+            jnp.logical_or(p >= FH, has_left), jnp.logical_or(p < FH + cx, has_right)
+        )
+        keep = jnp.where(inside, 1.0, 0.0)
+        coef[1, p] = diag + coef[0, p] * (1.0 / 7.0)
+        coef[2, p] = keep / jnp.where(inside, diag, 1.0)
+
+    factors = cheb_factors(FINE_STEPS)
+    last = FH + cx
+    planes_loop((FH + 1, last - 1, 2), diag_step)
+    get_force.wait()
+    start_sweep((FH + 1, last - 1, 2), src, coef, d, va, wa)
+    sweep(fine, (FH + 2, last - 2, 2), factors[0], src, coef, d, va, wa, vb, wb)
+    sweep(fine, (FH + 3, last - 3, 2), factors[1], src, coef, d, vb, wb, va, wa)
+
+    land(coef_pair)
+    planes_loop([1, last - 1, FH], diag_step)
+    land(force_pair)
+    start_sweep([1, last - 1, FH], src, coef, d, va, wa)
+    sweep(fine, [2, last - 2, FH], factors[0], src, coef, d, va, wa, vb, wb)
+    sweep(fine, [3, last - 3, FH], factors[1], src, coef, d, vb, wb, va, wa)
+
+    def residual_step(p):
+        image = fine.apply(va, wa, coef, p)
+        for c in range(3):
+            part = src[c, p] - image[c]
+            res[c, p - FH] = part
+            hi, lo = split(part)
+            at = pl.ds(pl.multiple_of((p - FH) * ny, ny), ny)
+            wide[0, c, at, :] = hi
+            wide[1, c, at, :] = lo
+
+    planes_loop((FH, last, 2), residual_step)
+
+    def pick(owner):
+        lanes = lane_table[owner]
+        live = live_table[owner]
+        hi = wide[0].reshape(3 * rows_f, nz)
+        lo = wide[1].reshape(3 * rows_f, nz)
+        found = jnp.dot(hi, lanes, preferred_element_type=F32) + jnp.dot(
+            lo, lanes, preferred_element_type=F32
+        )
+        rows = [
+            jnp.sum(found[c * rows_f : (c + 1) * rows_f] * live, axis=0, keepdims=True)
+            for c in range(3)
+        ]
+        return jnp.concatenate(rows + [jnp.zeros((5, slots), F32)], axis=0)
+
+    def a_copy(k):
+        owner = lax.rem(me + k, n)
+        return pltpu.make_async_remote_copy(
+            src_ref=sendbuf.at[owner], dst_ref=arrived.at[me],
+            send_sem=a_send.at[k], recv_sem=a_recv.at[k],
+            device_id={"space": owner}, device_id_type=MESH,
+        )
+
+    def pick_and_send(k, carry):
+        owner = lax.rem(me + k, n)
+        sendbuf[owner] = pick(owner)
+        a_copy(k).start()
+        return carry
+
+    lax.fori_loop(1, n, pick_and_send, 0)
+    arrived[me] = pick(me)
 
     pool = (
         lax.shift_right_logical(lax.broadcasted_iota(jnp.int32, (nz, hz), 0), 1)
@@ -280,20 +393,6 @@
 
     def pool_rows(i):
         return pooled[i, pl.ds(0, hy, stride=2), :] + pooled[i, pl.ds(1, hy, stride=2), :]
-
-    land(coef_pair)
-    kview = coef.at[0]
-
-    def diag_step(p):
-        diag = fine.diag(kview, p)
-        inside = jnp.logical_and(
-            jnp.logical_or(p >= FH, has_left), jnp.logical_or(p < FH + cx, has_right)
-        )
-        keep = jnp.where(inside, 1.0, 0.0)
-        coef[1, p] = diag + coef[0, p] * (1.0 / 7.0)
-        coef[2, p] = keep / jnp.where(inside, diag, 1.0)
-
-    planes_loop(1, top - 1, 1, diag_step)
 
     count_c = hx + 2
     first = FH - 2
@@ -310,66 +409,6 @@
         ccoef[2, CH + i] = 1.0 / diag
     start(ccoef_pair)
 
-    get_force.wait()
-    land(force_pair)
-
-    factors = cheb_factors(FINE_STEPS)
-    start_sweep(1, top - 1, 2, src, coef, d, va, wa)
-    sweep(fine, 2, top - 2, 1, factors[0], src, coef, d, va, wa, vb, wb)
-    sweep(fine, 3, top - 3, 1, factors[1], src, coef, d, vb, wb, va, wa)
-
-    def residual_step(p):
-        image = fine.apply(va, wa, coef, p)
-        for c in range(3):
-            res[c, p - FH] = src[c, p] - image[c]
-
-    planes_loop(FH, FH + cx, 1, residual_step)
-
-    rows_f = cx * ny
-    flat = res[...].reshape(3 * rows_f, nz)
-    flat_hi, flat_lo = split(flat)
-    wide[0] = flat_hi
-    wide[1] = flat_lo
-    zbits = nz.bit_length() - 1
-    hbits = hz.bit_length() - 1
-    sub_z = lax.broadcasted_iota(jnp.int32, (nz, slots), 0)
-    sub_r = lax.broadcasted_iota(jnp.int32, (rows_f, slots), 0)
-    slot_r = lax.broadcasted_iota(jnp.int32, (rows_f, slots), 1)
-
-    def pick(owner):
-        index = face_src[0, pl.ds(owner, 1), :]
-        lanes = (sub_z == jnp.bitwise_and(index, nz - 1)).astype(F32).astype(BF16)
-        found = jnp.dot(wide[0], lanes, preferred_element_type=F32) + jnp.dot(
-            wide[1], lanes, preferred_element_type=F32
-        )
-        live = jnp.logical_and(
-            sub_r == lax.shift_right_logical(index, zbits), slot_r < count[0, owner]
-        )
-        return [
-            jnp.sum(
-                jnp.where(live, found[c * rows_f : (c + 1) * rows_f], 0.0), axis=0, keepdims=True
-            )
-            for c in range(3)
-        ]
-
-    def a_copy(k):
-        owner = lax.rem(me + k, n)
-        return pltpu.make_async_remote_copy(
-            src_ref=sendbuf.at[owner], dst_ref=arrived.at[me],
-            send_sem=a_send.at[k], recv_sem=a_recv.at[k],
-            device_id={"space": owner}, device_id_type=MESH,
-        )
-
-    zero_tail = jnp.zeros((5, slots), F32)
-
-    @pl.loop(1, n)
-    def _(k):
-        owner = lax.rem(me + k, n)
-        sendbuf[owner] = jnp.concatenate(pick(owner) + [zero_tail], axis=0)
-        a_copy(k).start()
-
-    arrived[me] = jnp.concatenate(pick(me) + [zero_tail], axis=0)
-
     for c in range(3):
         stack = jnp.concatenate([res[c, 2 * i] + res[c, 2 * i + 1] for i in range(hx)], axis=0)
         pooled[0:hx] = dot2(stack, pool).reshape(hx, ny, hz)
@@ -377,12 +416,11 @@
             csrc[c, CH + i] = pool_rows(i) * 0.5
 
     rows_c = hx * hy
-    sub_l = lax.broadcasted_iota(jnp.int32, (hz, slots), 0)
     sub_c = lax.broadcasted_iota(jnp.int32, (rows_c, slots), 0)
 
     def place(sender):
         index = face_dst[0, pl.ds(sender, 1), :]
-        lanes = (sub_l == jnp.bitwise_and(index, hz - 1)).astype(F32).astype(BF16)
+        lanes = dst_table[sender]
         at_row = sub_c == lax.shift_right_logical(index, hbits)
         values = arrived[sender]
         parts = [jnp.where(at_row, values[c : c + 1], 0.0) for c in range(3)]
@@ -392,21 +430,26 @@
             lo, lanes, dims, preferred_element_type=F32
         )
 
+    total = place(me)
+
+    @pl.loop(1, n)
+    def _(k):
+        a_copy(k).wait_recv()
+
     def add_sender(k, total):
-        a_copy(k).wait_recv()
         return total + place(lax.rem(me + n - k, n))
 
-    total = lax.fori_loop(1, n, add_sender, place(me))
+    total = lax.fori_loop(1, n, add_sender, total, unroll=min(n - 1, 7))
     csrc[:, CH : CH + hx] += total.reshape(3, hx, hy, hz)
     start(csrc_pair)
     land(ccoef_pair)
     land(csrc_pair)
 
     factors = cheb_factors(COARSE_STEPS)
-    start_sweep(0, ctop, 2, csrc, ccoef, cd, cva, cwa)
-    sweep(coarse, 1, ctop - 1, 2, factors[0], csrc, ccoef, cd, cva, cwa, cvb, cwb)
-    sweep(coarse, 2, ctop - 2, 2, factors[1], csrc, ccoef, cd, cvb, cwb, cva, cwa)
-    sweep(coarse, 3, ctop - 3, 2, factors[2], csrc, ccoef, cd, cva, cwa, cvb, cwb)
+    start_sweep((0, ctop, ctop), csrc, ccoef, cd, cva, cwa)
+    sweep(coarse, (1, ctop - 1, ctop - 2), factors[0], csrc, ccoef, cd, cva, cwa, cvb, cwb)
+    sweep(coarse, (2, ctop - 2, ctop - 4), factors[1], csrc, ccoef, cd, cvb, cwb, cva, cwa)
+    sweep(coarse, (3, ctop - 3, ctop - 6), factors[2], csrc, ccoef, cd, cva, cwa, cvb, cwb)
 
     fresh = hx + 2
     for c in range(3):
@@ -432,7 +475,7 @@
         for i in range(loads):
             esend[i, p - FH] = energy[i * part : (i + 1) * part]
 
-    planes_loop(FH, FH + cx, 1, energy_step)
+    planes_loop((FH, FH + cx, 2), energy_step)
 
     def e_copy(k):
         owner = lax.rem(load + k, loads)
@@ -475,8 +518,7 @@
     fine = (cx + 2 * FH, ny, nz)
     coarse = (hx + 2 * CH, hy, hz)
     vmem = pl.BlockSpec(memory_space=pltpu.VMEM)
-    smem = pl.BlockSpec(memory_space=pltpu.SMEM)
-    hbm = pl.BlockSpec(memory_space=pl.ANY)
+    hbm = pl.BlockSpec(memory_space=pltpu.HBM)
 
     def buf(*shape):
         return pltpu.VMEM(shape, F32)
@@ -488,7 +530,7 @@
             jax.ShapeDtypeStruct(load_force.shape, F32),
             jax.ShapeDtypeStruct((3, cx, part, nz), F32),
         ),
-        in_specs=[hbm, hbm, smem, vmem, smem, vmem],
+        in_specs=[hbm] * 6,
         out_specs=(hbm, vmem),
         scratch_shapes=[
             buf(3, *fine), buf(cx, ny, nz), buf(3, *fine), buf(3, *fine),
@@ -496,14 +538,18 @@
             buf(3, cx, ny, nz), buf(hx + 2, ny, hz), buf(hx + 2, hy, hz),
             buf(3, *coarse), buf(3, *coarse), buf(3, *coarse),
             buf(3, *coarse), buf(3, *coarse), buf(3, *coarse), buf(3, *coarse),
-            pltpu.VMEM((2, 3 * cx * ny, nz), BF16),
+            pltpu.SMEM(material.shape, jnp.int32), pltpu.VMEM(face_src.shape, jnp.int32),
+            pltpu.SMEM(face_count.shape, jnp.int32), pltpu.VMEM(face_dst.shape, jnp.int32),
+            pltpu.VMEM((n, nz, slots), BF16), buf(n, cx * ny, slots),
+            pltpu.VMEM((n, hz, slots), BF16),
+            pltpu.VMEM((2, 3, cx * ny, nz), BF16),
             buf(n, 8, slots), buf(n, 8, slots),
             buf(loads, cx, part, nz), buf(loads, cx, part, nz),
-            dma((3,)), dma((4, 2)), dma((4, 2)),
+            dma((7,)), dma((4, 2)), dma((4, 2)),
             dma((n,)), dma((n,)), dma((loads,)), dma((loads,)),
         ],
         compiler_params=pltpu.CompilerParams(
-            collective_id=0, has_side_effects=True, vmem_limit_bytes=40 * 1024 * 1024
+            collective_id=0, has_side_effects=True, vmem_limit_bytes=60 * 1024 * 1024
         ),
     )(load_force, stiffness, material, face_src, face_count, face_dst)
 

time: 37.7 us -> 30.9 us (0.82)
  local copies, waits for them, and re-layouts: 5.98 us -> 2.45 us
  Pallas kernels: 30.7 us -> 27.7 us
    unnamed x14 -> x4, local copies, waits for them, and re-layouts: 5.98 us -> 2.45 us
    pallas_call x1, Pallas kernels: 30.7 us -> 27.7 us  [body(): pl.pallas_call(functools.partial(kernel, n, loads), out_shape=(jax.ShapeD...]
where the time goes in v2:
time: 30.9 us; the launch traced here: 30.8 us
  Pallas kernels  27.7 us (90%)
  local copies, waits for them, and re-layouts  2.45 us (8%)
  between operations  0.65 us (2%)
    pallas_call x1, Pallas kernels, body(): pl.pallas_call(functools.partial(kernel, n, loads), out_shape=(jax.ShapeD...  27.7 us
    unnamed x4, local copies, waits for them, and re-layouts  2.45 us

profile of v2, /device:TPU:1, one launch (start us, length us, event | category | flops | bytes accessed | tf_op | source)
XLA Modules:
  0.0 30.8 jit_solution(2719631830338573508)
XLA Ops:
  0.6 27.7 %shard_map.77 = (f32[1,3,8,16,256]{4,3,2,1,0:T(8,128)}, f32[3,8,4,256]{3,2,1,0:T(4,128)}) custom-call(f32[1,3,8,16,256]{4,3,2,1,0:T(8,128)} %force.1, f32[8,16,256]{2,1,0:T(8,128)} %stiff.1, s32[1,2]{1,0:T(1,128)} %mat_hbm.1, s32[1,8,256]{2,1,0:T(8,128)} %face_src_hbm.1, s32[1,8]{1,0:T(1,128)} %count_hbm.1, s32[1,8,256]{2,1,0:T(8,128)} %face_dst_hbm.1), custom_call_target="tpu_custom_call" | custom-call | tf_op jit(solution)/shard_map/pallas_call | solution.py:527
  28.3 0.0 copy-start
  28.3 1.8 %copy.10 = f32[1,3,8,16,256]{4,3,2,1,0:T(8,128)} copy(f32[1,3,8,16,256]{4,3,2,1,0:T(8,128)} %get-tuple-element.4) | data formatting | bytes 786432
  30.1 0.0 copy-done
  30.1 0.6 %copy.11 = f32[3,8,4,256]{3,2,1,0:T(4,128)} copy(f32[3,8,4,256]{3,2,1,0:T(4,128)S(1)} %copy-done) | data formatting | bytes 196608
Async XLA Ops:
  28.3 1.8 %copy-start = (f32[3,8,4,256]{3,2,1,0:T(4,128)S(1)}, f32[3,8,4,256]{3,2,1,0:T(4,128)}, u32[]{:S(2)}) copy-start(f32[3,8,4,256]{3,2,1,0:T(4,128)} %get-tuple-element.5) | copy-start | bytes 294916

commit v3 on v2

--- a/solution.py
+++ b/solution.py
@@ -49,22 +49,43 @@
 
 class Plane:
     def __init__(self, rows, lanes):
-        self.rows, self.lanes = rows, lanes
-        row = lax.broadcasted_iota(jnp.int32, (rows, lanes), 0)
-        lane = lax.broadcasted_iota(jnp.int32, (rows, lanes), 1)
-        self.masks = (row == rows - 1, row == 0, lane == lanes - 1, lane == 0)
+        self.sizes = (rows, lanes)
+        self.masks = []
+        for axis, other in ((0, lanes), (1, rows)):
+            shape = (8, other) if axis == 0 else (other, 128)
+            place = lax.broadcasted_iota(jnp.int32, shape, axis)
+            self.masks.append((place == shape[axis] - 1, place == 0))
+
+    def shift(self, a, axis, up):
+        tile = (8, 128)[axis]
+        count = self.sizes[axis] // tile
+        mask = self.masks[axis][0 if up else 1]
+        turned = [
+            pltpu.roll(
+                lax.slice_in_dim(a, i * tile, (i + 1) * tile, axis=axis),
+                tile - 1 if up else 1,
+                axis,
+            )
+            for i in range(count)
+        ]
+        out = []
+        for i in range(count):
+            near = i + 1 if up else i - 1
+            fill = turned[near] if 0 <= near < count else 0.0
+            out.append(jnp.where(mask, fill, turned[i]))
+        return out[0] if count == 1 else jnp.concatenate(out, axis=axis)
 
     def yp(self, a):
-        return jnp.where(self.masks[0], 0.0, pltpu.roll(a, self.rows - 1, 0))
+        return self.shift(a, 0, True)
 
     def ym(self, a):
-        return jnp.where(self.masks[1], 0.0, pltpu.roll(a, 1, 0))
+        return self.shift(a, 0, False)
 
     def zp(self, a):
-        return jnp.where(self.masks[2], 0.0, pltpu.roll(a, self.lanes - 1, 1))
+        return self.shift(a, 1, True)
 
     def zm(self, a):
-        return jnp.where(self.masks[3], 0.0, pltpu.roll(a, 1, 1))
+        return self.shift(a, 1, False)
 
     def ty(self, a):
         return a + 0.5 * (self.yp(a) + self.ym(a))
@@ -304,7 +325,9 @@
         sub_r = lax.broadcasted_iota(jnp.int32, (rows_f, slots), 0)
         slot_r = lax.broadcasted_iota(jnp.int32, (rows_f, slots), 1)
         index = face_src[0, pl.ds(owner, 1), :]
-        lane_table[owner] = (sub_z == jnp.bitwise_and(index, nz - 1)).astype(F32).astype(BF16)
+        lanes = (sub_z == jnp.bitwise_and(index, nz - 1)).astype(F32).astype(BF16)
+        lane_table[owner, 0:nz] = lanes
+        lane_table[owner, nz : 2 * nz] = lanes
         live = jnp.logical_and(
             sub_r == lax.shift_right_logical(index, zbits), slot_r < count[0, owner]
         )
@@ -346,18 +369,15 @@
             res[c, p - FH] = part
             hi, lo = split(part)
             at = pl.ds(pl.multiple_of((p - FH) * ny, ny), ny)
-            wide[0, c, at, :] = hi
-            wide[1, c, at, :] = lo
+            wide[c, at, 0:nz] = hi
+            wide[c, at, nz : 2 * nz] = lo
 
     planes_loop((FH, last, 2), residual_step)
 
     def pick(owner):
-        lanes = lane_table[owner]
         live = live_table[owner]
-        hi = wide[0].reshape(3 * rows_f, nz)
-        lo = wide[1].reshape(3 * rows_f, nz)
-        found = jnp.dot(hi, lanes, preferred_element_type=F32) + jnp.dot(
-            lo, lanes, preferred_element_type=F32
+        found = jnp.dot(
+            wide[...].reshape(3 * rows_f, 2 * nz), lane_table[owner], preferred_element_type=F32
         )
         rows = [
             jnp.sum(found[c * rows_f : (c + 1) * rows_f] * live, axis=0, keepdims=True)
@@ -373,14 +393,21 @@
             device_id={"space": owner}, device_id_type=MESH,
         )
 
-    def pick_and_send(k, carry):
-        owner = lax.rem(me + k, n)
-        sendbuf[owner] = pick(owner)
-        a_copy(k).start()
-        return carry
-
-    lax.fori_loop(1, n, pick_and_send, 0)
-    arrived[me] = pick(me)
+    group = 4 if n % 4 == 0 else 1
+
+    @pl.loop(0, n // group)
+    def _(i):
+        ks = [i * group + 1 + j for j in range(group)]
+        picked = [pick(lax.rem(me + k, n)) for k in ks]
+        for k, values in zip(ks, picked):
+            sendbuf[lax.rem(me + k, n)] = values
+        for k in ks:
+
+            @pl.when(k < n)
+            def _(k=k):
+                a_copy(k).start()
+
+    arrived[me] = sendbuf[me]
 
     pool = (
         lax.shift_right_logical(lax.broadcasted_iota(jnp.int32, (nz, hz), 0), 1)
@@ -475,18 +502,22 @@
         for i in range(loads):
             esend[i, p - FH] = energy[i * part : (i + 1) * part]
 
-    planes_loop((FH, FH + cx, 2), energy_step)
-
-    def e_copy(k):
+    halves = 2
+    chunk = cx // halves
+
+    def e_copy(k, half):
         owner = lax.rem(load + k, loads)
         return pltpu.make_async_remote_copy(
-            src_ref=esend.at[owner], dst_ref=erecv.at[k],
-            send_sem=e_send.at[k], recv_sem=e_recv.at[k],
+            src_ref=esend.at[owner, pl.ds(half * chunk, chunk)],
+            dst_ref=erecv.at[k, pl.ds(half * chunk, chunk)],
+            send_sem=e_send.at[k, half], recv_sem=e_recv.at[k, half],
             device_id={"load": owner}, device_id_type=MESH,
         )
 
-    for k in range(1, loads):
-        e_copy(k).start()
+    for half in range(halves):
+        planes_loop((FH + half * chunk, FH + (half + 1) * chunk, 2), energy_step)
+        for k in range(1, loads):
+            e_copy(k, half).start()
 
     sent(force_pair)
     sent(coef_pair)
@@ -497,17 +528,31 @@
     def _(k):
         a_copy(k).wait_send()
 
-    total = esend[load]
-    for k in range(1, loads):
-        e_copy(k).wait_recv()
-        total = total + erecv[k]
     brick = (load * part) // BY
-    for m, modulus in enumerate(MODULI):
-        ratio = by_material(brick, [(modulus - own) / own for own in MODULI])
-        sens_out[m] = total * ratio
-    for k in range(1, loads):
-        e_copy(k).wait_send()
+    ratios = [by_material(brick, [(modulus - own) / own for own in MODULI]) for modulus in MODULI]
     put_disp.wait()
+    for half in range(halves):
+        rows = slice(half * chunk, (half + 1) * chunk)
+        total = esend[load, rows]
+        for k in range(1, loads):
+            e_copy(k, half).wait_recv()
+            total = total + erecv[k, rows]
+        for m in range(len(MODULI)):
+            sens_out[m, rows] = total * ratios[m]
+    for half in range(halves):
+        for k in range(1, loads):
+            e_copy(k, half).wait_send()
+
+
+def deliver(disp, sens, disp_out, sens_out, sems):
+    copies = [
+        pltpu.make_async_copy(disp.at[0, c], disp_out.at[0, c], sems.at[c]) for c in range(3)
+    ]
+    copies.append(pltpu.make_async_copy(sens, sens_out, sems.at[3]))
+    for copy in copies:
+        copy.start()
+    for copy in copies:
+        copy.wait()
 
 
 def body(n, loads, load_force, stiffness, material, face_src, face_count, face_dst):
@@ -524,7 +569,7 @@
         return pltpu.VMEM(shape, F32)
 
     dma = pltpu.SemaphoreType.DMA
-    return pl.pallas_call(
+    disp, sens = pl.pallas_call(
         functools.partial(kernel, n, loads),
         out_shape=(
             jax.ShapeDtypeStruct(load_force.shape, F32),
@@ -540,18 +585,29 @@
             buf(3, *coarse), buf(3, *coarse), buf(3, *coarse), buf(3, *coarse),
             pltpu.SMEM(material.shape, jnp.int32), pltpu.VMEM(face_src.shape, jnp.int32),
             pltpu.SMEM(face_count.shape, jnp.int32), pltpu.VMEM(face_dst.shape, jnp.int32),
-            pltpu.VMEM((n, nz, slots), BF16), buf(n, cx * ny, slots),
+            pltpu.VMEM((n, 2 * nz, slots), BF16), buf(n, cx * ny, slots),
             pltpu.VMEM((n, hz, slots), BF16),
-            pltpu.VMEM((2, 3, cx * ny, nz), BF16),
+            pltpu.VMEM((3, cx * ny, 2 * nz), BF16),
             buf(n, 8, slots), buf(n, 8, slots),
             buf(loads, cx, part, nz), buf(loads, cx, part, nz),
             dma((7,)), dma((4, 2)), dma((4, 2)),
-            dma((n,)), dma((n,)), dma((loads,)), dma((loads,)),
+            dma((n,)), dma((n,)), dma((loads, 2)), dma((loads, 2)),
         ],
         compiler_params=pltpu.CompilerParams(
             collective_id=0, has_side_effects=True, vmem_limit_bytes=60 * 1024 * 1024
         ),
     )(load_force, stiffness, material, face_src, face_count, face_dst)
+    return pl.pallas_call(
+        deliver,
+        out_shape=(
+            jax.ShapeDtypeStruct(disp.shape, F32),
+            jax.ShapeDtypeStruct(sens.shape, F32),
+        ),
+        in_specs=[hbm] * 2,
+        out_specs=(hbm, hbm),
+        scratch_shapes=[dma((4,))],
+        compiler_params=pltpu.CompilerParams(vmem_limit_bytes=60 * 1024 * 1024),
+    )(disp, sens)
 
 
 def solution(mesh):

time: 30.9 us -> 44 us (1.42)
  Pallas kernels: 27.7 us -> 43.2 us
  local copies, waits for them, and re-layouts: 2.45 us -> 0 us
    pallas_call x0 -> x1, Pallas kernels: none -> 16 us  [body(): pl.pallas_call(deliver, out_shape=(jax.ShapeDtypeStruct(disp.shape, F32),...]
    unnamed x4 -> x0, local copies, waits for them, and re-layouts: 2.45 us -> none
    pallas_call x1, Pallas kernels: 27.7 us -> 27.2 us  [body(): pl.pallas_call(functools.partial(kernel, n, loads), out_shape=(jax.ShapeD...]
where the time goes in v3:
time: 44 us; the launch traced here: 43.9 us
  Pallas kernels  43.2 us (98%)
  between operations  0.64 us (1%)
    pallas_call x1, Pallas kernels, body(): pl.pallas_call(functools.partial(kernel, n, loads), out_shape=(jax.ShapeD...  27.2 us
    pallas_call x1, Pallas kernels, body(): pl.pallas_call(deliver, out_shape=(jax.ShapeDtypeStruct(disp.shape, F32),...  16 us

profile of v3, /device:TPU:1, one launch (start us, length us, event | category | flops | bytes accessed | tf_op | source)
XLA Modules:
  0.0 43.9 jit_solution(4241614991513130488)
XLA Ops:
  0.6 27.2 %shard_map.77 = (f32[1,3,8,16,256]{4,3,2,1,0:T(8,128)}, f32[3,8,4,256]{3,2,1,0:T(4,128)}) custom-call(f32[1,3,8,16,256]{4,3,2,1,0:T(8,128)} %force.1, f32[8,16,256]{2,1,0:T(8,128)} %stiff.1, s32[1,2]{1,0:T(1,128)} %mat_hbm.1, s32[1,8,256]{2,1,0:T(8,128)} %face_src_hbm.1, s32[1,8]{1,0:T(1,128)} %count_hbm.1, s32[1,8,256]{2,1,0:T(8,128)} %face_dst_hbm.1), custom_call_target="tpu_custom_call" | custom-call | tf_op jit(solution)/shard_map/pallas_call | solution.py:572
  27.8 16.0 %shard_map.78 = (f32[1,3,8,16,256]{4,3,2,1,0:T(8,128)}, f32[3,8,4,256]{3,2,1,0:T(4,128)}) custom-call(f32[1,3,8,16,256]{4,3,2,1,0:T(8,128)} %get-tuple-element.4.disp, f32[3,8,4,256]{3,2,1,0:T(4,128)} %get-tuple-element.5.sens), custom_call_target="tpu_custom_call" | custom-call | tf_op jit(solution)/shard_map/pallas_call | solution.py:600

commit v4 on v3

--- a/solution.py
+++ b/solution.py
@@ -176,8 +176,8 @@
     n, loads,
     force, stiff, mat_hbm, face_src_hbm, count_hbm, face_dst_hbm,
     disp_out, sens_out,
-    src, raw, coef, d, va, wa, vb, wb, res, pooled, kc, ccoef, csrc, cd, cva, cwa, cvb, cwb,
-    mat, face_src, count, face_dst, lane_table, live_table, dst_table,
+    src, raw, coef, d, va, wa, vb, wb, res, pooled, kc, kcx, ccoef, csrc, cd, cva, cwa, cvb, cwb,
+    lift, mat, face_src, count, face_dst, lane_table, live_table, dst_table,
     wide, sendbuf, arrived, esend, erecv,
     local_sem, send_sem, recv_sem, a_send, a_recv, e_send, e_recv,
 ):
@@ -233,21 +233,26 @@
             )
         return made
 
-    fw = FH - 1
-    force_pair = pair(
+    far = FH - 2
+    near_pair = pair(
         0,
-        (force.at[0, :, pl.ds(cx - fw, fw)], src.at[:, pl.ds(1, fw)]),
-        (force.at[0, :, pl.ds(0, fw)], src.at[:, pl.ds(FH + cx, fw)]),
+        (src.at[:, pl.ds(FH + cx - 1, 1)], src.at[:, pl.ds(FH - 1, 1)]),
+        (src.at[:, pl.ds(FH, 1)], src.at[:, pl.ds(FH + cx, 1)]),
+    )
+    far_pair = pair(
+        4,
+        (src.at[:, pl.ds(FH + cx - 1 - far, far)], src.at[:, pl.ds(1, far)]),
+        (src.at[:, pl.ds(FH + 1, far)], src.at[:, pl.ds(FH + cx + 1, far)]),
     )
     coef_pair = pair(
         1,
         (coef.at[0, pl.ds(cx, FH)], coef.at[0, pl.ds(0, FH)]),
         (coef.at[0, pl.ds(FH, FH)], coef.at[0, pl.ds(FH + cx, FH)]),
     )
-    ccoef_pair = pair(
+    kc_pair = pair(
         2,
-        (ccoef.at[:, pl.ds(CH, hx)], ccoef.at[:, pl.ds(0, hx)]),
-        (ccoef.at[:, pl.ds(CH, hx)], ccoef.at[:, pl.ds(CH + hx, hx)]),
+        (kc.at[pl.ds(0, hx + 1)], kcx.at[pl.ds(0, hx + 1)]),
+        (kc.at[pl.ds(1, hx + 1)], kcx.at[pl.ds(CH + 1 + hx, hx + 1)]),
     )
     csrc_pair = pair(
         3,
@@ -287,14 +292,14 @@
     def _():
         src[:, 0:FH] = jnp.zeros((3, FH, ny, nz), F32)
         coef[0, 0:FH] = jnp.zeros((FH, ny, nz), F32)
-        ccoef[:, 0:CH] = jnp.zeros((3, CH, hy, hz), F32)
+        kcx[0 : CH + 1] = jnp.zeros((CH + 1, hy, hz), F32)
         csrc[:, 0:CH] = jnp.zeros((3, CH, hy, hz), F32)
 
     @pl.when(me == n - 1)
     def _():
         src[:, FH + cx : top] = jnp.zeros((3, FH, ny, nz), F32)
         coef[0, FH + cx : top] = jnp.zeros((FH, ny, nz), F32)
-        ccoef[:, CH + hx : ctop] = jnp.zeros((3, CH, hy, hz), F32)
+        kcx[CH + 1 + hx : ctop + 2] = jnp.zeros((CH + 1, hy, hz), F32)
         csrc[:, CH + hx : ctop] = jnp.zeros((3, CH, hy, hz), F32)
 
     def by_material(brick, values):
@@ -308,9 +313,11 @@
         rows = slice(brick * BY, (brick + 1) * BY)
         coef[0, FH : FH + cx, rows] = raw[:, rows] * own
 
+    get_force.wait()
     pl.semaphore_wait(barrier, n - 1 + loads - 1)
     start(coef_pair)
-    start(force_pair)
+    start(near_pair)
+    start(far_pair)
 
     rows_f = cx * ny
     zbits = nz.bit_length() - 1
@@ -350,17 +357,21 @@
     factors = cheb_factors(FINE_STEPS)
     last = FH + cx
     planes_loop((FH + 1, last - 1, 2), diag_step)
-    get_force.wait()
     start_sweep((FH + 1, last - 1, 2), src, coef, d, va, wa)
     sweep(fine, (FH + 2, last - 2, 2), factors[0], src, coef, d, va, wa, vb, wb)
     sweep(fine, (FH + 3, last - 3, 2), factors[1], src, coef, d, vb, wb, va, wa)
 
-    land(coef_pair)
-    planes_loop([1, last - 1, FH], diag_step)
-    land(force_pair)
-    start_sweep([1, last - 1, FH], src, coef, d, va, wa)
-    sweep(fine, [2, last - 2, FH], factors[0], src, coef, d, va, wa, vb, wb)
-    sweep(fine, [3, last - 3, FH], factors[1], src, coef, d, vb, wb, va, wa)
+    pool = (
+        lax.shift_right_logical(lax.broadcasted_iota(jnp.int32, (nz, hz), 0), 1)
+        == lax.broadcasted_iota(jnp.int32, (nz, hz), 1)
+    ).astype(F32).astype(BF16)
+    spread = (
+        lax.shift_right_logical(lax.broadcasted_iota(jnp.int32, (hz, nz), 1), 1)
+        == lax.broadcasted_iota(jnp.int32, (hz, nz), 0)
+    ).astype(F32).astype(BF16)
+
+    def pool_rows(i):
+        return pooled[i, pl.ds(0, hy, stride=2), :] + pooled[i, pl.ds(1, hy, stride=2), :]
 
     def residual_step(p):
         image = fine.apply(va, wa, coef, p)
@@ -372,7 +383,30 @@
             wide[c, at, 0:nz] = hi
             wide[c, at, nz : 2 * nz] = lo
 
-    planes_loop((FH, last, 2), residual_step)
+    land(coef_pair)
+    planes_loop([1, last - 1, FH], diag_step)
+
+    count_c = hx + 2
+    first = FH - 2
+    stack = jnp.concatenate(
+        [coef[0, first + 2 * i] + coef[0, first + 2 * i + 1] for i in range(count_c)], axis=0
+    )
+    pooled[0:count_c] = dot2(stack, pool).reshape(count_c, ny, hz)
+    for i in range(count_c):
+        kc[i] = pool_rows(i) * 0.125
+    kcx[CH + 1 : CH + 1 + hx] = kc[1 : 1 + hx]
+
+    land(near_pair)
+    start_sweep([3, last - 1, 2], src, coef, d, va, wa)
+    sweep(fine, [4, last - 2, 2], factors[0], src, coef, d, va, wa, vb, wb)
+    sweep(fine, [5, last - 3, 2], factors[1], src, coef, d, vb, wb, va, wa)
+    planes_loop([6, last - 4, 2], residual_step)
+    land(far_pair)
+    start_sweep([1, last + 1, 2], src, coef, d, va, wa)
+    sweep(fine, [2, last, 2], factors[0], src, coef, d, va, wa, vb, wb)
+    sweep(fine, [3, last - 1, 2], factors[1], src, coef, d, vb, wb, va, wa)
+    planes_loop([4, last - 2, 2], residual_step)
+    start(kc_pair)
 
     def pick(owner):
         live = live_table[owner]
@@ -383,7 +417,7 @@
             jnp.sum(found[c * rows_f : (c + 1) * rows_f] * live, axis=0, keepdims=True)
             for c in range(3)
         ]
-        return jnp.concatenate(rows + [jnp.zeros((5, slots), F32)], axis=0)
+        return jnp.concatenate(rows, axis=0)
 
     def a_copy(k):
         owner = lax.rem(me + k, n)
@@ -408,33 +442,6 @@
                 a_copy(k).start()
 
     arrived[me] = sendbuf[me]
-
-    pool = (
-        lax.shift_right_logical(lax.broadcasted_iota(jnp.int32, (nz, hz), 0), 1)
-        == lax.broadcasted_iota(jnp.int32, (nz, hz), 1)
-    ).astype(F32).astype(BF16)
-    spread = (
-        lax.shift_right_logical(lax.broadcasted_iota(jnp.int32, (hz, nz), 1), 1)
-        == lax.broadcasted_iota(jnp.int32, (hz, nz), 0)
-    ).astype(F32).astype(BF16)
-
-    def pool_rows(i):
-        return pooled[i, pl.ds(0, hy, stride=2), :] + pooled[i, pl.ds(1, hy, stride=2), :]
-
-    count_c = hx + 2
-    first = FH - 2
-    stack = jnp.concatenate(
-        [coef[0, first + 2 * i] + coef[0, first + 2 * i + 1] for i in range(count_c)], axis=0
-    )
-    pooled[0:count_c] = dot2(stack, pool).reshape(count_c, ny, hz)
-    for i in range(count_c):
-        kc[i] = pool_rows(i) * 0.125
-    for i in range(hx):
-        diag = coarse.diag(kc, i + 1)
-        ccoef[0, CH + i] = kc[i + 1]
-        ccoef[1, CH + i] = diag + kc[i + 1] * (1.0 / 7.0)
-        ccoef[2, CH + i] = 1.0 / diag
-    start(ccoef_pair)
 
     for c in range(3):
         stack = jnp.concatenate([res[c, 2 * i] + res[c, 2 * i + 1] for i in range(hx)], axis=0)
@@ -469,7 +476,20 @@
     total = lax.fori_loop(1, n, add_sender, total, unroll=min(n - 1, 7))
     csrc[:, CH : CH + hx] += total.reshape(3, hx, hy, hz)
     start(csrc_pair)
-    land(ccoef_pair)
+    land(kc_pair)
+    for p in range(ctop):
+        diag = coarse.diag(kcx, p + 1)
+        k = kcx[p + 1]
+        ccoef[0, p] = k
+        ccoef[1, p] = diag + k * (1.0 / 7.0)
+        if p < CH:
+            keep = jnp.where(has_left, 1.0, 0.0)
+            ccoef[2, p] = keep / jnp.where(has_left, diag, 1.0)
+        elif p >= CH + hx:
+            keep = jnp.where(has_right, 1.0, 0.0)
+            ccoef[2, p] = keep / jnp.where(has_right, diag, 1.0)
+        else:
+            ccoef[2, p] = 1.0 / diag
     land(csrc_pair)
 
     factors = cheb_factors(COARSE_STEPS)
@@ -483,11 +503,18 @@
         lifted = dot2(cvb[c, 3 : 3 + fresh].reshape(fresh * hy, hz), spread)
         for i in range(fresh):
             plane = lifted[i * hy : (i + 1) * hy]
-            doubled = jnp.broadcast_to(plane[:, None, :], (hy, 2, nz)).reshape(ny, nz)
+            for h in range(nz // 128):
+                part = plane[:, h * 128 : (h + 1) * 128]
+                lift[c, i, h, pl.ds(0, hy, stride=2), :] = part
+                lift[c, i, h, pl.ds(1, hy, stride=2), :] = part
+    for c in range(3):
+        for i in range(fresh):
+            doubled = jnp.concatenate([lift[c, i, h] for h in range(nz // 128)], axis=1)
             for p in (FH - 2 + 2 * i, FH - 1 + 2 * i):
                 if FH - 1 <= p <= FH + cx:
-                    vb[c, p] = va[c, p] + doubled
-                    wb[c, p] = coef[0, p] * vb[c, p]
+                    moved = va[c, p] + doubled
+                    vb[c, p] = moved
+                    wb[c, p] = coef[0, p] * moved
 
     put_disp = pltpu.make_async_copy(
         vb.at[:, pl.ds(FH, cx)], disp_out.at[0], local_sem.at[2]
@@ -519,9 +546,10 @@
         for k in range(1, loads):
             e_copy(k, half).start()
 
-    sent(force_pair)
+    sent(near_pair)
+    sent(far_pair)
     sent(coef_pair)
-    sent(ccoef_pair)
+    sent(kc_pair)
     sent(csrc_pair)
 
     @pl.loop(1, n)
@@ -544,14 +572,21 @@
             e_copy(k, half).wait_send()
 
 
-def deliver(disp, sens, disp_out, sens_out, sems):
-    copies = [
-        pltpu.make_async_copy(disp.at[0, c], disp_out.at[0, c], sems.at[c]) for c in range(3)
+def deliver(disp, sens, disp_out, sens_out, disp_buf, sens_buf, sems):
+    pieces = [(disp.at[0, c], disp_buf.at[c], disp_out.at[0, c]) for c in range(3)]
+    pieces += [(sens.at[m], sens_buf.at[m], sens_out.at[m]) for m in range(3)]
+    ins = [
+        pltpu.make_async_copy(a, b, sems.at[0, i]) for i, (a, b, _) in enumerate(pieces)
     ]
-    copies.append(pltpu.make_async_copy(sens, sens_out, sems.at[3]))
-    for copy in copies:
+    outs = [
+        pltpu.make_async_copy(b, c, sems.at[1, i]) for i, (_, b, c) in enumerate(pieces)
+    ]
+    for copy in ins:
         copy.start()
-    for copy in copies:
+    for arriving, leaving in zip(ins, outs):
+        arriving.wait()
+        leaving.start()
+    for copy in outs:
         copy.wait()
 
 
@@ -581,16 +616,17 @@
             buf(3, *fine), buf(cx, ny, nz), buf(3, *fine), buf(3, *fine),
             buf(3, *fine), buf(3, *fine), buf(3, *fine), buf(3, *fine),
             buf(3, cx, ny, nz), buf(hx + 2, ny, hz), buf(hx + 2, hy, hz),
-            buf(3, *coarse), buf(3, *coarse), buf(3, *coarse),
+            buf(hx + 2 * CH + 2, hy, hz), buf(3, *coarse), buf(3, *coarse), buf(3, *coarse),
             buf(3, *coarse), buf(3, *coarse), buf(3, *coarse), buf(3, *coarse),
+            buf(3, hx + 2, nz // 128, ny, 128),
             pltpu.SMEM(material.shape, jnp.int32), pltpu.VMEM(face_src.shape, jnp.int32),
             pltpu.SMEM(face_count.shape, jnp.int32), pltpu.VMEM(face_dst.shape, jnp.int32),
             pltpu.VMEM((n, 2 * nz, slots), BF16), buf(n, cx * ny, slots),
             pltpu.VMEM((n, hz, slots), BF16),
             pltpu.VMEM((3, cx * ny, 2 * nz), BF16),
-            buf(n, 8, slots), buf(n, 8, slots),
+            buf(n, 3, slots), buf(n, 3, slots),
             buf(loads, cx, part, nz), buf(loads, cx, part, nz),
-            dma((7,)), dma((4, 2)), dma((4, 2)),
+            dma((7,)), dma((5, 2)), dma((5, 2)),
             dma((n,)), dma((n,)), dma((loads, 2)), dma((loads, 2)),
         ],
         compiler_params=pltpu.CompilerParams(
@@ -605,7 +641,7 @@
         ),
         in_specs=[hbm] * 2,
         out_specs=(hbm, hbm),
-        scratch_shapes=[dma((4,))],
+        scratch_shapes=[buf(*disp.shape[1:]), buf(*sens.shape), dma((2, 6))],
         compiler_params=pltpu.CompilerParams(vmem_limit_bytes=60 * 1024 * 1024),
     )(disp, sens)
 

time: 44 us -> 28.5 us (0.65)
  Pallas kernels: 43.2 us -> 27.7 us
    pallas_call x1, Pallas kernels: 16 us -> 1.82 us  [body(): pl.pallas_call(deliver, out_shape=(jax.ShapeDtypeStruct(disp.shape, F32),...]
    pallas_call x1, Pallas kernels: 27.2 us -> 25.9 us  [body(): pl.pallas_call(functools.partial(kernel, n, loads), out_shape=(jax.ShapeD...]
where the time goes in v4:
time: 28.5 us; the launch traced here: 28.3 us
  Pallas kernels  27.7 us (97%)
  between operations  0.64 us (2%)
    pallas_call x1, Pallas kernels, body(): pl.pallas_call(functools.partial(kernel, n, loads), out_shape=(jax.ShapeD...  25.9 us
    pallas_call x1, Pallas kernels, body(): pl.pallas_call(deliver, out_shape=(jax.ShapeDtypeStruct(disp.shape, F32),...  1.82 us

profile of v4, /device:TPU:1, one launch (start us, length us, event | category | flops | bytes accessed | tf_op | source)
XLA Modules:
  0.0 28.3 jit_solution(4629606541687466208)
XLA Ops:
  0.6 25.9 %shard_map.77 = (f32[1,3,8,16,256]{4,3,2,1,0:T(8,128)}, f32[3,8,4,256]{3,2,1,0:T(4,128)}) custom-call(f32[1,3,8,16,256]{4,3,2,1,0:T(8,128)} %force.1, f32[8,16,256]{2,1,0:T(8,128)} %stiff.1, s32[1,2]{1,0:T(1,128)} %mat_hbm.1, s32[1,8,256]{2,1,0:T(8,128)} %face_src_hbm.1, s32[1,8]{1,0:T(1,128)} %count_hbm.1, s32[1,8,256]{2,1,0:T(8,128)} %face_dst_hbm.1), custom_call_target="tpu_custom_call" | custom-call | tf_op jit(solution)/shard_map/pallas_call | solution.py:607
  26.5 1.8 %shard_map.78 = (f32[1,3,8,16,256]{4,3,2,1,0:T(8,128)}, f32[3,8,4,256]{3,2,1,0:T(4,128)}) custom-call(f32[1,3,8,16,256]{4,3,2,1,0:T(8,128)} %get-tuple-element.4.disp, f32[3,8,4,256]{3,2,1,0:T(4,128)} %get-tuple-element.5.sens), custom_call_target="tpu_custom_call" | custom-call | tf_op jit(solution)/shard_map/pallas_call | solution.py:636

commit v5 on v4

--- a/solution.py
+++ b/solution.py
@@ -221,72 +221,104 @@
     right = lax.rem(me + 1, n)
     left = lax.rem(me + n - 1, n)
 
-    def pair(kind, to_right, to_left):
-        made = []
-        for side, (ends, target) in enumerate(((to_right, right), (to_left, left))):
-            made.append(
-                pltpu.make_async_remote_copy(
-                    src_ref=ends[0], dst_ref=ends[1],
-                    send_sem=send_sem.at[kind, side], recv_sem=recv_sem.at[kind, side],
-                    device_id={"space": target}, device_id_type=MESH,
+    def pairs(base, ends):
+        made = ([], [])
+        for piece, ways in enumerate(ends):
+            for side, ((at, to), target) in enumerate(zip(ways, (right, left))):
+                made[side].append(
+                    pltpu.make_async_remote_copy(
+                        src_ref=at, dst_ref=to,
+                        send_sem=send_sem.at[base + piece, side],
+                        recv_sem=recv_sem.at[base + piece, side],
+                        device_id={"space": target}, device_id_type=MESH,
+                    )
                 )
+        return made
+
+    far = FH - 2
+    coef_pair = pairs(
+        0,
+        [
+            (
+                (coef.at[0, pl.ds(cx + i, 2)], coef.at[0, pl.ds(i, 2)]),
+                (coef.at[0, pl.ds(FH + i, 2)], coef.at[0, pl.ds(FH + cx + i, 2)]),
             )
-        return made
-
-    far = FH - 2
-    near_pair = pair(
-        0,
-        (src.at[:, pl.ds(FH + cx - 1, 1)], src.at[:, pl.ds(FH - 1, 1)]),
-        (src.at[:, pl.ds(FH, 1)], src.at[:, pl.ds(FH + cx, 1)]),
-    )
-    far_pair = pair(
-        4,
-        (src.at[:, pl.ds(FH + cx - 1 - far, far)], src.at[:, pl.ds(1, far)]),
-        (src.at[:, pl.ds(FH + 1, far)], src.at[:, pl.ds(FH + cx + 1, far)]),
-    )
-    coef_pair = pair(
-        1,
-        (coef.at[0, pl.ds(cx, FH)], coef.at[0, pl.ds(0, FH)]),
-        (coef.at[0, pl.ds(FH, FH)], coef.at[0, pl.ds(FH + cx, FH)]),
-    )
-    kc_pair = pair(
+            for i in range(0, FH, 2)
+        ],
+    )
+    near_pair = pairs(
         2,
-        (kc.at[pl.ds(0, hx + 1)], kcx.at[pl.ds(0, hx + 1)]),
-        (kc.at[pl.ds(1, hx + 1)], kcx.at[pl.ds(CH + 1 + hx, hx + 1)]),
-    )
-    csrc_pair = pair(
-        3,
-        (csrc.at[:, pl.ds(CH, hx)], csrc.at[:, pl.ds(0, hx)]),
-        (csrc.at[:, pl.ds(CH, hx)], csrc.at[:, pl.ds(CH + hx, hx)]),
+        [
+            (
+                (src.at[c, pl.ds(FH + cx - 1, 1)], src.at[c, pl.ds(FH - 1, 1)]),
+                (src.at[c, pl.ds(FH, 1)], src.at[c, pl.ds(FH + cx, 1)]),
+            )
+            for c in range(3)
+        ],
+    )
+    far_pair = pairs(
+        5,
+        [
+            (
+                (src.at[c, pl.ds(FH + cx - 1 - far, far)], src.at[c, pl.ds(1, far)]),
+                (src.at[c, pl.ds(FH + 1, far)], src.at[c, pl.ds(FH + cx + 1, far)]),
+            )
+            for c in range(3)
+        ],
+    )
+    kc_pair = pairs(
+        8,
+        [
+            (
+                (kc.at[pl.ds(0, hx + 1)], kcx.at[pl.ds(0, hx + 1)]),
+                (kc.at[pl.ds(1, hx + 1)], kcx.at[pl.ds(CH + 1 + hx, hx + 1)]),
+            )
+        ],
+    )
+    csrc_pair = pairs(
+        9,
+        [
+            (
+                (csrc.at[c, pl.ds(CH, hx)], csrc.at[c, pl.ds(0, hx)]),
+                (csrc.at[c, pl.ds(CH, hx)], csrc.at[c, pl.ds(CH + hx, hx)]),
+            )
+            for c in range(3)
+        ],
     )
     has_left, has_right = me > 0, me < n - 1
 
     def start(made):
         @pl.when(has_right)
         def _():
-            made[0].start()
+            for copy in made[0]:
+                copy.start()
 
         @pl.when(has_left)
         def _():
-            made[1].start()
+            for copy in made[1]:
+                copy.start()
 
     def land(made):
         @pl.when(has_left)
         def _():
-            made[0].wait_recv()
+            for copy in made[0]:
+                copy.wait_recv()
 
         @pl.when(has_right)
         def _():
-            made[1].wait_recv()
+            for copy in made[1]:
+                copy.wait_recv()
 
     def sent(made):
         @pl.when(has_right)
         def _():
-            made[0].wait_send()
+            for copy in made[0]:
+                copy.wait_send()
 
         @pl.when(has_left)
         def _():
-            made[1].wait_send()
+            for copy in made[1]:
+                copy.wait_send()
 
     @pl.when(me == 0)
     def _():
@@ -626,7 +658,7 @@
             pltpu.VMEM((3, cx * ny, 2 * nz), BF16),
             buf(n, 3, slots), buf(n, 3, slots),
             buf(loads, cx, part, nz), buf(loads, cx, part, nz),
-            dma((7,)), dma((5, 2)), dma((5, 2)),
+            dma((7,)), dma((12, 2)), dma((12, 2)),
             dma((n,)), dma((n,)), dma((loads, 2)), dma((loads, 2)),
         ],
         compiler_params=pltpu.CompilerParams(

time: 28.5 us -> 28.7 us (level)
  no operation moved by 1% of the time
where the time goes in v5:
time: 28.7 us; the launch traced here: 28.6 us
  Pallas kernels  27.9 us (97%)
  between operations  0.64 us (2%)
    pallas_call x1, Pallas kernels, body(): pl.pallas_call(functools.partial(kernel, n, loads), out_shape=(jax.ShapeD...  26.1 us
    pallas_call x1, Pallas kernels, body(): pl.pallas_call(deliver, out_shape=(jax.ShapeDtypeStruct(disp.shape, F32),...  1.82 us

profile of v5, /device:TPU:1, one launch (start us, length us, event | category | flops | bytes accessed | tf_op | source)
XLA Modules:
  0.0 28.6 jit_solution(1397192361557903847)
XLA Ops:
  0.6 26.1 %shard_map.77 = (f32[1,3,8,16,256]{4,3,2,1,0:T(8,128)}, f32[3,8,4,256]{3,2,1,0:T(4,128)}) custom-call(f32[1,3,8,16,256]{4,3,2,1,0:T(8,128)} %force.1, f32[8,16,256]{2,1,0:T(8,128)} %stiff.1, s32[1,2]{1,0:T(1,128)} %mat_hbm.1, s32[1,8,256]{2,1,0:T(8,128)} %face_src_hbm.1, s32[1,8]{1,0:T(1,128)} %count_hbm.1, s32[1,8,256]{2,1,0:T(8,128)} %face_dst_hbm.1), custom_call_target="tpu_custom_call" | custom-call | tf_op jit(solution)/shard_map/pallas_call | solution.py:639
  26.8 1.8 %shard_map.78 = (f32[1,3,8,16,256]{4,3,2,1,0:T(8,128)}, f32[3,8,4,256]{3,2,1,0:T(4,128)}) custom-call(f32[1,3,8,16,256]{4,3,2,1,0:T(8,128)} %get-tuple-element.4.disp, f32[3,8,4,256]{3,2,1,0:T(4,128)} %get-tuple-element.5.sens), custom_call_target="tpu_custom_call" | custom-call | tf_op jit(solution)/shard_map/pallas_call | solution.py:668

commit v6 on v4

--- a/solution.py
+++ b/solution.py
@@ -514,12 +514,9 @@
                 if FH - 1 <= p <= FH + cx:
                     moved = va[c, p] + doubled
                     vb[c, p] = moved
+                    if FH <= p < FH + cx:
+                        disp_out[0, c, p - FH] = moved
                     wb[c, p] = coef[0, p] * moved
-
-    put_disp = pltpu.make_async_copy(
-        vb.at[:, pl.ds(FH, cx)], disp_out.at[0], local_sem.at[2]
-    )
-    put_disp.start()
 
     part = ny // loads
 
@@ -558,7 +555,6 @@
 
     brick = (load * part) // BY
     ratios = [by_material(brick, [(modulus - own) / own for own in MODULI]) for modulus in MODULI]
-    put_disp.wait()
     for half in range(halves):
         rows = slice(half * chunk, (half + 1) * chunk)
         total = esend[load, rows]
@@ -572,21 +568,14 @@
             e_copy(k, half).wait_send()
 
 
-def deliver(disp, sens, disp_out, sens_out, disp_buf, sens_buf, sems):
-    pieces = [(disp.at[0, c], disp_buf.at[c], disp_out.at[0, c]) for c in range(3)]
-    pieces += [(sens.at[m], sens_buf.at[m], sens_out.at[m]) for m in range(3)]
-    ins = [
-        pltpu.make_async_copy(a, b, sems.at[0, i]) for i, (a, b, _) in enumerate(pieces)
+def deliver(disp, sens, disp_out, sens_out, sems):
+    copies = [
+        pltpu.make_async_copy(disp.at[0, c], disp_out.at[0, c], sems.at[c]) for c in range(3)
     ]
-    outs = [
-        pltpu.make_async_copy(b, c, sems.at[1, i]) for i, (_, b, c) in enumerate(pieces)
-    ]
-    for copy in ins:
+    copies.append(pltpu.make_async_copy(sens, sens_out, sems.at[3]))
+    for copy in copies:
         copy.start()
-    for arriving, leaving in zip(ins, outs):
-        arriving.wait()
-        leaving.start()
-    for copy in outs:
+    for copy in copies:
         copy.wait()
 
 
@@ -607,11 +596,11 @@
     disp, sens = pl.pallas_call(
         functools.partial(kernel, n, loads),
         out_shape=(
-            jax.ShapeDtypeStruct(load_force.shape, F32),
-            jax.ShapeDtypeStruct((3, cx, part, nz), F32),
+            pltpu.VMEM(load_force.shape, F32),
+            pltpu.VMEM((3, cx, part, nz), F32),
         ),
         in_specs=[hbm] * 6,
-        out_specs=(hbm, vmem),
+        out_specs=(vmem, vmem),
         scratch_shapes=[
             buf(3, *fine), buf(cx, ny, nz), buf(3, *fine), buf(3, *fine),
             buf(3, *fine), buf(3, *fine), buf(3, *fine), buf(3, *fine),
@@ -639,10 +628,10 @@
             jax.ShapeDtypeStruct(disp.shape, F32),
             jax.ShapeDtypeStruct(sens.shape, F32),
         ),
-        in_specs=[hbm] * 2,
+        in_specs=[vmem] * 2,
         out_specs=(hbm, hbm),
-        scratch_shapes=[buf(*disp.shape[1:]), buf(*sens.shape), dma((2, 6))],
-        compiler_params=pltpu.CompilerParams(vmem_limit_bytes=60 * 1024 * 1024),
+        scratch_shapes=[dma((4,))],
+        compiler_params=pltpu.CompilerParams(vmem_limit_bytes=4 * 1024 * 1024),
     )(disp, sens)
 
 

time: 28.5 us -> 26.8 us (0.940)
  Pallas kernels: 27.7 us -> 26.1 us
    pallas_call x1, Pallas kernels: 1.82 us -> 0.81 us  [body(): pl.pallas_call(deliver, out_shape=(jax.ShapeDtypeStruct(disp.shape, F32),...]
    pallas_call x1, Pallas kernels: 25.9 us -> 25.2 us  [body(): pl.pallas_call(functools.partial(kernel, n, loads), out_shape=(pltpu.VMEM...]
where the time goes in v6:
time: 26.8 us; the launch traced here: 26.7 us
  Pallas kernels  26.1 us (97%)
  between operations  0.64 us (2%)
    pallas_call x1, Pallas kernels, body(): pl.pallas_call(functools.partial(kernel, n, loads), out_shape=(pltpu.VMEM...  25.2 us
    pallas_call x1, Pallas kernels, body(): pl.pallas_call(deliver, out_shape=(jax.ShapeDtypeStruct(disp.shape, F32),...  0.81 us

profile of v6, /device:TPU:1, one launch (start us, length us, event | category | flops | bytes accessed | tf_op | source)
XLA Modules:
  0.0 26.7 jit_solution(13492149761991574417)
XLA Ops:
  0.6 25.2 %shard_map.77 = (f32[1,3,8,16,256]{4,3,2,1,0:T(8,128)S(1)}, f32[3,8,4,256]{3,2,1,0:T(4,128)S(1)}) custom-call(f32[1,3,8,16,256]{4,3,2,1,0:T(8,128)} %force.1, f32[8,16,256]{2,1,0:T(8,128)} %stiff.1, s32[1,2]{1,0:T(1,128)} %mat_hbm.1, s32[1,8,256]{2,1,0:T(8,128)} %face_src_hbm.1, s32[1,8]{1,0:T(1,128)} %count_hbm.1, s32[1,8,256]{2,1,0:T(8,128)} %face_dst_hbm.1), custom_call_target="tpu_custom_call" | custom-call | tf_op jit(solution)/shard_map/pallas_call | solution.py:596
  25.9 0.8 %shard_map.78 = (f32[1,3,8,16,256]{4,3,2,1,0:T(8,128)}, f32[3,8,4,256]{3,2,1,0:T(4,128)}) custom-call(f32[1,3,8,16,256]{4,3,2,1,0:T(8,128)S(1)} %get-tuple-element.4.disp, f32[3,8,4,256]{3,2,1,0:T(4,128)S(1)} %get-tuple-element.5.sens), custom_call_target="tpu_custom_call" | custom-call | tf_op jit(solution)/shard_map/pallas_call | solution.py:625
